TPU v7x, 32 devices: a whole 2x2x4 slice. The times are simulated.
32 devices in a mesh: dp: 8 (over z, y), mp: 4 (over x, core).
Axes of the slice: x: 2, y: 2, z: 4, core: 2. Of those that a mesh axis runs over, the one named last changes fastest.
Arguments:
- tokens: bfloat16 [16384, 1024], P(('dp', 'mp')), may hold values from -6 to 6
- counts: int32 [8], P('dp'), may hold values from 1024 to 2048, as said below
- gain_attn: float32 [1024], replicated, may hold values from 0.5 to 1.5
- gain_ffn: float32 [1024], replicated, may hold values from 0.5 to 1.5
- w_qkv: bfloat16 [1024, 3, 1024], P(None, None, 'mp'), may hold values from -0.1875 to 0.1875
- w_out: bfloat16 [1024, 1024], P('mp'), may hold values from -2 to 2
- w_gate_up: bfloat16 [1024, 2, 2816], P(None, None, 'mp'), may hold values from -0.1875 to 0.1875
- w_down: bfloat16 [2816, 1024], P('mp'), may hold values from -0.109375 to 0.109375
- cotangent: bfloat16 [16384, 1024], P(('dp', 'mp')), may hold values from -6 to 6
Outputs:
- latents: float32 [16384, 1024], P(('dp', 'mp'))
- grad_tokens: float32 [16384, 1024], P(('dp', 'mp'))
- grad_gain_attn: float32 [1024], replicated
- grad_gain_ffn: float32 [1024], replicated
- grad_w_qkv: float32 [1024, 3, 1024], P(None, None, 'mp')
- grad_w_out: float32 [1024, 1024], P('mp')
- grad_w_gate_up: float32 [1024, 2, 2816], P(None, None, 'mp')
- grad_w_down: float32 [2816, 1024], P('mp')
Inputs may be any that keep to these rules, and one draw needn't show every extreme that they name: `counts`: number of real patches of each sequence; the rest of its 2048 slots are padding. Some sequence has exactly 2048 and some exactly 1024.
All inputs are finite; a program needn't handle non-finite values.
Results may differ from a plain program's by a relative error of at most 0.015.
Values may be sent and summed in bfloat16 or wider, within the bound.
No kernel may reach another device: no remote copies, remote signals or barrier semaphores. Data moves between devices by JAX's collectives and lax.ppermute only.
A program may use at most 192 MiB of HBM per device.

v0:
```python
import jax
import jax.numpy as jnp
from jax import lax
from jax.sharding import PartitionSpec as P

HD = 64


EPS = 1e-05


def rms_scale(values, gain):
    return values * lax.rsqrt(jnp.mean(values * values, axis=-1, keepdims=True) + EPS) * gain


def allowed_mask(first, last, patch_count):
    row_pos = first + jnp.arange(last - first, dtype=jnp.int32)[:, None]
    col_pos = jnp.arange(last, dtype=jnp.int32)[None, :]
    return (col_pos <= row_pos) & (col_pos < patch_count)


def block_scores(queries, keys, first, last, patch_count, scale):
    scores = (
        jnp.einsum(
            "qhd,khd->hqk", queries[first:last], keys[:last], preferred_element_type=jnp.float32
        )
        * scale
    )
    return jnp.where(allowed_mask(first, last, patch_count)[None], scores, -1e30)


def attend_forward(queries, keys, values, patch_count, scale):
    length = queries.shape[0]
    block = min(512, length)
    outputs = []
    log_parts = []
    for first in range(0, length, block):
        last = first + block
        scores = block_scores(queries, keys, first, last, patch_count, scale)
        peak = jnp.max(scores, axis=-1, keepdims=True)
        expo = jnp.exp(scores - peak)
        total = jnp.sum(expo, axis=-1, keepdims=True)
        probs_low = (expo / total).astype(jnp.bfloat16)
        outputs.append(
            jnp.einsum("hqk,khd->qhd", probs_low, values[:last], preferred_element_type=jnp.float32)
        )
        log_parts.append(peak + jnp.log(total))
    return (jnp.concatenate(outputs, axis=0), jnp.concatenate(log_parts, axis=1))


def attend_backward(queries, keys, values, grad_out, log_totals, patch_count, scale):
    length = queries.shape[0]
    block = min(512, length)
    grad_keys = jnp.zeros(keys.shape, jnp.float32)
    grad_values = jnp.zeros(values.shape, jnp.float32)
    query_parts = []
    for first in range(0, length, block):
        last = first + block
        scores = block_scores(queries, keys, first, last, patch_count, scale)
        probs = jnp.exp(scores - log_totals[:, first:last])
        probs_low = probs.astype(jnp.bfloat16)
        out_block = grad_out[first:last]
        grad_values = grad_values.at[:last].add(
            jnp.einsum("hqk,qhd->khd", probs_low, out_block, preferred_element_type=jnp.float32)
        )
        grad_probs = jnp.einsum(
            "qhd,khd->hqk", out_block, values[:last], preferred_element_type=jnp.float32
        )
        inner = jnp.sum(grad_probs * probs, axis=-1, keepdims=True)
        grad_scores = (probs * (grad_probs - inner)).astype(jnp.bfloat16)
        query_parts.append(
            jnp.einsum("hqk,khd->qhd", grad_scores, keys[:last], preferred_element_type=jnp.float32)
            * scale
        )
        grad_keys = grad_keys.at[:last].add(
            jnp.einsum(
                "hqk,qhd->khd", grad_scores, queries[first:last], preferred_element_type=jnp.float32
            )
            * scale
        )
    return (jnp.concatenate(query_parts, axis=0), grad_keys, grad_values)


def on_device(tokens, counts, gain_attn, gain_ffn, w_qkv, w_out, w_gate_up, w_down, cotangent):
    width = tokens.shape[1]
    columns = w_qkv.shape[2]
    heads = columns // HD
    hidden_cols = w_gate_up.shape[2]
    scale = HD ** (-0.5)
    patch_count = counts[0]
    inputs = tokens.astype(jnp.float32)
    qkv_flat = w_qkv.reshape(width, 3 * columns)
    gate_up_flat = w_gate_up.reshape(width, 2 * hidden_cols)
    normed_attn = lax.all_gather(
        rms_scale(inputs, gain_attn).astype(jnp.bfloat16), "mp", axis=0, tiled=True
    )
    length = normed_attn.shape[0]
    projected = jnp.dot(normed_attn, qkv_flat, preferred_element_type=jnp.float32).astype(
        jnp.bfloat16
    )
    projected = projected.reshape(length, 3, heads, HD)
    queries = projected[:, 0]
    keys = projected[:, 1]
    values = projected[:, 2]
    mixed, log_totals = attend_forward(queries, keys, values, patch_count, scale)
    attended = mixed.reshape(length, columns).astype(jnp.bfloat16)
    piece = attended
    middle = inputs + lax.psum_scatter(
        jnp.dot(piece, w_out, preferred_element_type=jnp.float32),
        "mp",
        scatter_dimension=0,
        tiled=True,
    )
    normed_ffn = lax.all_gather(
        rms_scale(middle, gain_ffn).astype(jnp.bfloat16), "mp", axis=0, tiled=True
    )
    both = jnp.dot(normed_ffn, gate_up_flat, preferred_element_type=jnp.float32)
    gate = both[:, :hidden_cols]
    up = both[:, hidden_cols:]
    hidden = (jax.nn.silu(gate) * up).astype(jnp.bfloat16)
    piece = hidden
    latents = middle + lax.psum_scatter(
        jnp.dot(piece, w_down, preferred_element_type=jnp.float32).astype(jnp.bfloat16),
        "mp",
        scatter_dimension=0,
        tiled=True,
    ).astype(jnp.float32)
    upstream = cotangent.astype(jnp.float32)
    upstream_all = lax.all_gather(cotangent, "mp", axis=0, tiled=True)
    grad_w_down = jnp.einsum("rf,rd->fd", hidden, upstream_all, preferred_element_type=jnp.float32)
    grad_hidden = jnp.einsum("rd,fd->rf", upstream_all, w_down, preferred_element_type=jnp.float32)

    def swiglu(gate_in, up_in):
        return jax.nn.silu(gate_in) * up_in

    unused, swiglu_pull = jax.vjp(swiglu, gate, up)
    grad_gate, grad_up = swiglu_pull(grad_hidden)
    grad_both = jnp.concatenate([grad_gate, grad_up], axis=1).astype(jnp.bfloat16)
    grad_w_gate_up = jnp.einsum(
        "rd,rc->dc", normed_ffn, grad_both, preferred_element_type=jnp.float32
    ).reshape(width, 2, hidden_cols)
    piece = grad_both
    grad_normed_ffn = lax.psum_scatter(
        jnp.einsum("rc,dc->rd", piece, gate_up_flat, preferred_element_type=jnp.float32).astype(
            jnp.bfloat16
        ),
        "mp",
        scatter_dimension=0,
        tiled=True,
    ).astype(jnp.float32)
    unused, norm_pull = jax.vjp(rms_scale, middle, gain_ffn)
    grad_middle_norm, grad_gain_ffn = norm_pull(grad_normed_ffn)
    grad_middle = upstream + grad_middle_norm
    branch_grad = lax.all_gather(grad_middle.astype(jnp.bfloat16), "mp", axis=0, tiled=True)
    grad_w_out = jnp.einsum("rc,rd->cd", attended, branch_grad, preferred_element_type=jnp.float32)
    grad_attended = jnp.einsum("rd,cd->rc", branch_grad, w_out, preferred_element_type=jnp.float32)
    grad_attended = grad_attended.astype(jnp.bfloat16).reshape(length, heads, HD)
    grad_queries, grad_keys, grad_values = attend_backward(
        queries, keys, values, grad_attended, log_totals, patch_count, scale
    )
    grad_projected = jnp.stack([grad_queries, grad_keys, grad_values], axis=1)
    grad_projected = grad_projected.astype(jnp.bfloat16).reshape(length, 3 * columns)
    grad_w_qkv = jnp.einsum(
        "rd,rc->dc", normed_attn, grad_projected, preferred_element_type=jnp.float32
    ).reshape(width, 3, columns)
    piece = grad_projected
    grad_normed_attn = lax.psum_scatter(
        jnp.einsum("rc,dc->rd", piece, qkv_flat, preferred_element_type=jnp.float32).astype(
            jnp.bfloat16
        ),
        "mp",
        scatter_dimension=0,
        tiled=True,
    ).astype(jnp.float32)
    unused, first_pull = jax.vjp(rms_scale, inputs, gain_attn)
    grad_input_norm, grad_gain_attn = first_pull(grad_normed_attn)
    grad_tokens = grad_middle + grad_input_norm
    grad_w_qkv, grad_w_out, grad_w_gate_up, grad_w_down = lax.psum(
        (grad_w_qkv, grad_w_out, grad_w_gate_up, grad_w_down), "dp"
    )
    grad_gain_attn, grad_gain_ffn = lax.psum((grad_gain_attn, grad_gain_ffn), ("dp", "mp"))
    return (
        latents,
        grad_tokens,
        grad_gain_attn,
        grad_gain_ffn,
        grad_w_qkv,
        grad_w_out,
        grad_w_gate_up,
        grad_w_down,
    )


def solution(mesh):
    placed = (
        P(("dp", "mp"), None),
        P("dp"),
        P(),
        P(),
        P(None, None, "mp"),
        P("mp", None),
        P(None, None, "mp"),
        P("mp", None),
        P(("dp", "mp"), None),
    )
    return jax.shard_map(
        on_device,
        mesh=mesh,
        in_specs=placed,
        out_specs=(
            P(("dp", "mp"), None),
            P(("dp", "mp"), None),
            P(),
            P(),
            P(None, None, "mp"),
            P("mp", None),
            P(None, None, "mp"),
            P("mp", None),
        ),
        check_vma=False,
    )
```

profile of v0, /device:TPU:0, one launch (start us, length us, event | category | flops | bytes accessed | tf_op | source)
XLA Modules:
  0.0 988.1 jit_solution(4061987062729772031)
XLA Ops:
  20.4 29.6 %all-gather.5.cloned.1.call-done = bf16[2048,1024]{1,0:T(8,128)(2,1)} async-done(((bf16[512,1024]{1,0:T(8,128)(2,1)}), bf16[2048,1024]{1,0:T(8,128)(2,1)}) %all-gather.5.cloned.1.call-update) | async-done | bytes 4194320 | tf_op jit(solution)/shard_map/all_gather | solution.py:94
  77.7 7.5 fusion.109
  85.2 8.1 fusion
  93.4 8.2 fusion.94
  107.5 71.8 %reduce-scatter.5.cloned.1.call-done = f32[512,1024]{1,0:T(8,128)} async-done(((f32[2048,1024]{1,0:T(8,128)}), f32[512,1024]{1,0:T(8,128)}) %reduce-scatter.5.cloned.1.call-update) | async-done | bytes 2097168 | tf_op jit(solution)/shard_map/reduce_scatter | solution.py:108
  184.7 34.0 %all-gather.7.cloned.1.call-done = bf16[2048,1024]{1,0:T(8,128)(2,1)} async-done(((bf16[512,1024]{1,0:T(8,128)(2,1)}), bf16[2048,1024]{1,0:T(8,128)(2,1)}) %all-gather.7.cloned.1.call-update) | async-done | bytes 4194320 | tf_op jit(solution)/shard_map/all_gather | solution.py:114
  218.8 11.3 %fusion.114 = f32[2048,1408]{0,1:T(8,128)} fusion(bf16[2048,1024]{1,0:T(8,128)(2,1)} %all-gather.7.cloned.1.call-done, bf16[1024,1408]{0,1:T(8,128)(2,1)S(1)} %bitcast.193), kind=kOutput, calls=%fused_computation.180 | convolution fusion | flops 5905580032 | bytes 18612224 | tf_op jit(solution)/shard_map/dot_general | solution.py:117
  230.1 24.7 %all-gather.9.cloned.1.call-done = bf16[2048,1024]{1,0:T(8,128)(2,1)} async-done(((bf16[512,1024]{1,0:T(8,128)(2,1)}), bf16[2048,1024]{1,0:T(8,128)(2,1)}) %all-gather.9.cloned.1.call-update) | async-done | bytes 4194320 | tf_op jit(solution)/shard_map/all_gather | solution.py:129
  254.8 11.0 %fusion.16 = (bf16[2048,704]{0,1:T(8,128)(2,1)S(1)}, bf16[2048,704]{0,1:T(8,128)(2,1)S(1)}, bf16[2048,704]{0,1:T(8,128)(2,1)}) fusion(f32[2048,1408]{0,1:T(8,128)} %fusion.114, bf16[2048,1024]{1,0:T(8,128)(2,1)} %all-gather.9.cloned.1.call-done, bf16[704,1024]{1,0:T(8,128)(2,1)} %param.36), kind=kOutput, calls=%fused_computation.34 | convolution fusion | flops 2975858688 | bytes 25821184 | tf_op jit(solution)/shard_map/rd,fd->rf/dot_general | solution.py:131
  268.4 8.3 convolution_convert_fusion
  276.7 44.6 %reduce-scatter.9.cloned.1.call-done = bf16[512,1024]{1,0:T(8,128)(2,1)} async-done(((bf16[2048,1024]{1,0:T(8,128)(2,1)}), bf16[512,1024]{1,0:T(8,128)(2,1)}) %reduce-scatter.9.cloned.1.call-update) | async-done | bytes 1048592 | tf_op jit(solution)/shard_map/reduce_scatter | solution.py:143
  326.7 34.3 %all-gather.11.cloned.1.call-done = bf16[2048,1024]{1,0:T(8,128)(2,1)} async-done(((bf16[512,1024]{1,0:T(8,128)(2,1)}), bf16[2048,1024]{1,0:T(8,128)(2,1)}) %all-gather.11.cloned.1.call-update) | async-done | bytes 4194320 | tf_op jit(solution)/shard_map/all_gather | solution.py:154
  381.4 7.2 multiply_reduce_fusion.1
  391.4 11.3 %multiply_reduce_fusion = (f32[4,512]{1,0:T(4,128)S(1)}, f32[4,512,2048]{2,1,0:T(8,128)}) fusion(f32[4,512,2048]{2,1,0:T(8,128)} %get-tuple-element.142, f32[4,512]{1,0:T(4,128)S(1)} %log_add_fusion, bf16[512,4,64]{0,2,1:T(8,128)(2,1)S(1)} %bitcast.226, bf16[2048,3,4,64]{0,3,2,1:T(8,128)(2,1)} %bitcast.213), kind=kOutput, calls=%fused_computation.1 | convolution fusion | flops 549451776 | bytes 34881536 | tf_op jit(solution)/shard_map/qhd,khd->hqk/dot_general | solution.py:66
  402.7 8.6 fusion.50
  411.6 6.7 multiply_convert_fusion.2
  422.8 10.5 %multiply_convert_fusion.1 = bf16[4,512,1536]{2,1,0:T(8,128)(2,1)} fusion(f32[4,512,1536]{2,1,0:T(8,128)} %get-tuple-element.154, f32[4,512,1536]{2,1,0:T(8,128)S(1)} %bitcast.198, f32[4,512]{1,0:T(4,128)S(1)} %get-tuple-element.153, f32[4,512]{1,0:T(4,128)S(1)} %log_add_fusion.1), kind=kLoop, calls=%fused_computation.8 | loop fusion | flops 12582912 | bytes 31473664 | tf_op jit(solution)/shard_map/convert_element_type | solution.py:70
  442.6 7.7 multiply_convert_fusion
  464.3 7.8 convolution_convert_fusion.1
  472.4 8.7 fusion.116
  481.1 9.5 fusion.25
  499.4 9.5 reduce-scatter.11.cloned.1.call-done
  511.4 39.7 %all-reduce.2 = (f32[1024]{0:T(1024)}, f32[1024]{0:T(1024)}) all-reduce(f32[1024]{0:T(1024)S(1)} %get-tuple-element.122, f32[1024]{0:T(1024)S(1)} %get-tuple-element.120), channel_id=1, replica_groups=mesh['dp'=8,'mp'=4] {'dp','mp'}, use_global_device_ids=true, to_apply=%region_21.22 | all-reduce | flops 2048 | bytes 16384 | tf_op jit(solution)/shard_map/psum | solution.py:181
  561.3 409.3 %all-reduce.6.cloned.1.call-done = (f32[1024,3,256]{2,0,1:T(8,128)}, f32[256,1024]{1,0:T(8,128)}, f32[1024,2,704]{0,2,1:T(8,128)}, f32[704,1024]{1,0:T(8,128)}) async-done(((f32[1024,3,256]{2,0,1:T(8,128)}, f32[256,1024]{1,0:T(8,128)}, f32[1024,2,704]{0,2,1:T(8,128)}, f32[704,1024]{1,0:T(8,128)}), (f32[1024,3,256]{2,0,1:T(8,128)}, f32[256,1024]{1,0:T(8,128)}, f32[1024,2,704]{0,2,1:T(8,128)}, ...) | async-done | bytes 12845072 | tf_op jit(solution)/shard_map/psum | solution.py:178
  (187 shorter events, 142.6 us)
Async XLA Ops:
  7.2 211.6 %copy-start = (bf16[1024,2,704]{0,2,1:T(8,128)(2,1)S(1)}, bf16[1024,2,704]{0,2,1:T(8,128)(2,1)}, u32[]{:S(2)}) copy-start(bf16[1024,2,704]{0,2,1:T(8,128)(2,1)} %param.35) | copy-start | bytes 8650756
  7.2 42.7 %all-gather.5.cloned.1.call-start = ((), (), s32[]{:S(2)}) async-start(), calls=%async_computation.4 | async-start | bytes 5242880 | tf_op jit(solution)/shard_map/all_gather | solution.py:94
  12.6 166.8 %reduce-scatter.5.cloned.1.call-start = ((), (), s32[]{:S(2)}) async-start(), calls=%async_computation.5 | async-start | bytes 10485760 | tf_op jit(solution)/shard_map/reduce_scatter | solution.py:108
  56.1 9.8 copy-start.8
  93.4 9.4 copy-start.22
  107.5 75.4 %copy-start.27 = (f32[1024]{0:T(1024)S(1)}, f32[1024]{0:T(1024)}, u32[]{:S(2)}) copy-start(f32[1024]{0:T(1024)} %param.32) | copy-start | bytes 12292
  107.5 111.3 %all-gather.7.cloned.1.call-start = ((), (), s32[]{:S(2)}) async-start(), calls=%async_computation.6 | async-start | bytes 5242880 | tf_op jit(solution)/shard_map/all_gather | solution.py:114
  184.1 70.6 %all-gather.9.cloned.1.call-start = ((), (), s32[]{:S(2)}) async-start(), calls=%async_computation.8 | async-start | bytes 5242880 | tf_op jit(solution)/shard_map/all_gather | solution.py:129
  184.7 136.7 %reduce-scatter.9.cloned.1.call-start = ((), (), s32[]{:S(2)}) async-start(), calls=%async_computation.9 | async-start | bytes 5242880 | tf_op jit(solution)/shard_map/reduce_scatter | solution.py:143
  276.7 44.7 %copy-start.7 = (f32[512,1024]{1,0:T(8,128)S(1)}, f32[512,1024]{1,0:T(8,128)}, u32[]{:S(2)}) copy-start(f32[512,1024]{1,0:T(8,128)} %copy-done.6) | copy-start | bytes 6291460
  276.7 84.4 %all-gather.11.cloned.1.call-start = ((), (), s32[]{:S(2)}) async-start(), calls=%async_computation.10 | async-start | bytes 5242880 | tf_op jit(solution)/shard_map/all_gather | solution.py:154
  326.4 182.4 %reduce-scatter.11.cloned.1.call-start = ((), (), s32[]{:S(2)}) async-start(), calls=%async_computation.11 | async-start | bytes 5242880 | tf_op jit(solution)/shard_map/reduce_scatter | solution.py:167
  422.7 19.8 %slice-start = ((s8[16777216]{0:T(1024)(128)(4,1)}), s8[4194304]{0:T(1024)(128)(4,1)S(1)}, s32[]{:S(2)}) async-start(s8[16777216]{0:T(1024)(128)(4,1)} %bitcast.195), calls=%async_computation.13 | async-start | bytes 8388608
  422.8 19.8 %slice-start.1 = ((s8[16777216]{0:T(1024)(128)(4,1)}), s8[4194304]{0:T(1024)(128)(4,1)S(1)}, s32[]{:S(2)}) async-start(s8[16777216]{0:T(1024)(128)(4,1)} %bitcast.195), calls=%async_computation.14 | async-start | bytes 8388608
  422.8 19.8 %slice-start.2 = ((s8[16777216]{0:T(1024)(128)(4,1)}), s8[4194304]{0:T(1024)(128)(4,1)S(1)}, s32[]{:S(2)}) async-start(s8[16777216]{0:T(1024)(128)(4,1)} %bitcast.195), calls=%async_computation.15 | async-start | bytes 8388608
  433.2 9.3 slice-start.3
  464.2 92.6 %reduce-scatter.7.cloned.1.call-start = ((), (), s32[]{:S(2)}) async-start(), calls=%async_computation.7 | async-start | bytes 5242880 | tf_op jit(solution)/shard_map/reduce_scatter | solution.py:122
  472.1 498.5 %all-reduce.6.cloned.1.call-start = ((), (), s32[]{:S(2)}) async-start(), calls=%async_computation.12 | async-start | bytes 25690112 | tf_op jit(solution)/shard_map/psum | solution.py:178
  472.3 8.7 copy-start.34
  481.0 9.5 copy-start.12
  481.1 9.5 copy-start.35
  499.4 9.5 copy-start.28
  499.4 9.5 copy-start.30
  499.4 51.7 %copy-start.32 = (f32[512]{0:T(512)S(1)}, f32[512]{0:T(512)}, u32[]{:S(2)}) copy-start(f32[512]{0:T(512)} %copy-done.31) | copy-start | bytes 6148
  (34 other events, 152.9 us)
Sparse Core Ops, SparseCore 0:
  12.7 37.1 all-gather.4
  107.6 71.7 reduce-scatter.4
  184.2 34.4 all-gather.6
  220.2 34.4 all-gather.8
  276.8 44.5 reduce-scatter.8
  326.6 34.4 all-gather.10
  464.4 44.4 reduce-scatter.10
  511.6 45.2 reduce-scatter.6
  562.2 408.3 all-reduce.5
where the time goes:
time: 997 us; the launch traced here: 988 us
  waiting for transfers between devices  664 us (67%)
  matrix products  179 us (18%)
  other arithmetic  63.2 us (6%)
  blocking collectives  39.7 us (4%)
  local copies, waits for them, and re-layouts  26.1 us (3%)
  between operations  15.4 us (2%)
    psum x1, waiting for transfers between devices, on_device(): lax.psum((grad_w_qkv, grad_w_out, grad_w_gate_up, grad_w_down), 'dp')  409 us
    reduce_scatter x1, waiting for transfers between devices, on_device(): lax.psum_scatter(jnp.dot(piece, w_out, preferred_element_type=jnp.float32...  71.8 us
    reduce_scatter x1, waiting for transfers between devices, on_device(): lax.psum_scatter(jnp.einsum('rc,dc->rd', piece, gate_up_flat, preferred_e...  44.6 us
    psum x1, blocking collectives, on_device(): lax.psum((grad_gain_attn, grad_gain_ffn), ('dp', 'mp'))  39.7 us
    all_gather x1, waiting for transfers between devices, on_device(): lax.all_gather(grad_middle.astype(jnp.bfloat16), 'mp', axis=0, tiled=True)  34.3 us
    all_gather x1, waiting for transfers between devices, on_device(): lax.all_gather(rms_scale(middle, gain_ffn).astype(jnp.bfloat16), 'mp', ax...  34 us
    all_gather x1, waiting for transfers between devices, on_device(): lax.all_gather(rms_scale(inputs, gain_attn).astype(jnp.bfloat16), 'mp', a...  29.6 us
    convert_element_type x4, other arithmetic, attend_backward(): grad_scores = (probs * (grad_probs - inner)).astype(jnp.bfloat16)  26.2 us
  transfers between devices with their start and end apart: 9, of which 9 were waited for; matrix products, arithmetic and copies ran while one was open for 6% of the time, Pallas kernels for 0%

commit v1 on v0

v1 whole, which is shorter than its diff:
```python
import functools

import jax
import jax.numpy as jnp
from jax import lax
from jax.experimental import pallas as pl
from jax.experimental.pallas import tpu as pltpu
from jax.sharding import PartitionSpec as P

HD = 64


EPS = 1e-05


def rms_scale(values, gain):
    return values * lax.rsqrt(jnp.mean(values * values, axis=-1, keepdims=True) + EPS) * gain


LANES=128
LOG2E=1.4426950408889634
NT=(((1,),(1,)),((),()))
TN=(((0,),(0,)),((),()))
f32=jnp.float32; bf16=jnp.bfloat16

def dot(a,b,dims=(((1,),(0,)),((),()))):
    return lax.dot_general(a,b,dims,preferred_element_type=f32)

def head_lanes(rows, parity):
    lane=lax.broadcasted_iota(jnp.int32,(rows,LANES),1)
    return (lane//HD)==parity, lane==(1-parity)*HD

def attn_fwd_kernel(count_ref, qkv_ref, o_ref, lse_ref, kaug, *, length, columns, block):
    h=pl.program_id(0)
    parity=lax.rem(h,2)
    col=pl.multiple_of((h//2)*LANES,LANES)
    c=HD**-0.5*LOG2E
    sel,spare=head_lanes(length,parity)
    row=lax.broadcasted_iota(jnp.int32,(length,LANES),0)
    k=qkv_ref[:,pl.ds(columns+col,LANES)].astype(f32)
    bias=jnp.where(row<count_ref[0],0.0,-1e30)
    kaug[...]=jnp.where(sel,k,jnp.where(spare,bias,0.0)).astype(bf16)
    sel_b,spare_b=head_lanes(block,parity)
    ri=lax.broadcasted_iota(jnp.int32,(block,block),0)
    ci=lax.broadcasted_iota(jnp.int32,(block,block),1)
    for i in range(length//block):
        first=i*block; n=first+block
        rows=pl.ds(first,block)
        q=qkv_ref[rows,pl.ds(col,LANES)].astype(f32)
        q=jnp.where(sel_b,q,jnp.where(spare_b,1.0,0.0)).astype(bf16)
        s_d=dot(q,kaug[first:n],NT)
        s_d=jnp.where(ci<=ri,s_d,-1e30)
        m=jnp.max(s_d,axis=1,keepdims=True)
        if first:
            s_o=dot(q,kaug[:first],NT)
            m=jnp.maximum(m,jnp.max(s_o,axis=1,keepdims=True))
        mc=m*c
        p_d=jnp.exp2(s_d*c-mc)
        l=jnp.sum(p_d,axis=1,keepdims=True)
        v=qkv_ref[first:n,pl.ds(2*columns+col,LANES)]
        o=dot(p_d.astype(bf16),v)
        if first:
            p_o=jnp.exp2(s_o*c-mc)
            l=l+jnp.sum(p_o,axis=1,keepdims=True)
            o=o+dot(p_o.astype(bf16),qkv_ref[:first,pl.ds(2*columns+col,LANES)])
        o=(o/l).astype(bf16)
        out=pl.ds(col,LANES)
        prev=o_ref[rows,out]
        o_ref[rows,out]=jnp.where(sel_b,o,prev)
        lse=mc+jnp.log2(l)
        lse_ref[pl.ds(h,1),first:n]=jnp.transpose(jnp.broadcast_to(lse,(block,LANES)))[0:1]

def attn_fwd(count, qkv, block=256):
    length,three=qkv.shape; columns=three//3; heads=columns//HD
    return pl.pallas_call(
        functools.partial(attn_fwd_kernel,length=length,columns=columns,block=block),
        grid=(heads,),
        out_shape=(jax.ShapeDtypeStruct((length,columns),bf16),jax.ShapeDtypeStruct((heads,length),f32)),
        in_specs=[pl.BlockSpec(memory_space=pltpu.SMEM),pl.BlockSpec((length,three),lambda h:(0,0))],
        out_specs=(pl.BlockSpec((length,columns),lambda h:(0,0)),pl.BlockSpec((heads,length),lambda h:(0,0))),
        scratch_shapes=[pltpu.VMEM((length,LANES),bf16)],
        compiler_params=pltpu.CompilerParams(vmem_limit_bytes=50<<20),
        cost_estimate=pl.CostEstimate(flops=4*length*length*columns,bytes_accessed=2*length*columns*4,transcendentals=length*length*heads//2),
        name="attn_fwd",
    )(count,qkv)

def attn_bwd_kernel(count_ref, qkv_ref, do_ref, o_ref, lse_ref, g_ref, kaug, qaug, dom, dq, *, length, columns, block):
    h=pl.program_id(0)
    parity=lax.rem(h,2)
    col=pl.multiple_of((h//2)*LANES,LANES)
    scale=HD**-0.5
    c=scale*LOG2E
    sel,spare=head_lanes(length,parity)
    row=lax.broadcasted_iota(jnp.int32,(length,LANES),0)
    k=qkv_ref[:,pl.ds(columns+col,LANES)].astype(f32)
    bias=jnp.where(row<count_ref[0],0.0,-1e30)
    kaug[...]=jnp.where(sel,k,jnp.where(spare,bias,0.0)).astype(bf16)
    q=qkv_ref[:,pl.ds(col,LANES)].astype(f32)
    qaug[...]=jnp.where(sel,q,jnp.where(spare,1.0,0.0)).astype(bf16)
    do=jnp.where(sel,do_ref[:,pl.ds(col,LANES)].astype(f32),0.0)
    dom[...]=do.astype(bf16)
    prod=do*o_ref[:,pl.ds(col,LANES)].astype(f32)
    hi=prod.astype(bf16)
    lo=(prod-hi.astype(f32)).astype(bf16)
    ones=jnp.ones((8,LANES),bf16)
    delta=(dot(ones,hi,NT)+dot(ones,lo,NT))[0:1]
    lse=lse_ref[pl.ds(h,1),:]
    sel_b,_=head_lanes(block,parity)
    ki=lax.broadcasted_iota(jnp.int32,(block,block),0)
    qi=lax.broadcasted_iota(jnp.int32,(block,block),1)
    dq[...]=jnp.zeros_like(dq)
    for j in range(length//block):
        first=j*block; last=first+block
        kj=kaug[first:last]
        vj=qkv_ref[first:last,pl.ds(2*columns+col,LANES)]
        def part(a,b,diag):
            s=dot(kj,qaug[a:b],NT)
            if diag: s=jnp.where(ki<=qi,s,-1e30)
            p=jnp.exp2(s*c-lse[:,a:b])
            dp=dot(vj,dom[a:b],NT)
            ds=(p*(dp-delta[:,a:b])).astype(bf16)
            pb=p.astype(bf16)
            dv=dot(pb,dom[a:b])
            dk=dot(ds,qaug[a:b])
            dq[a:b]+=dot(ds,kj,TN)
            return dv,dk
        dv,dk=part(first,last,True)
        if last<length:
            dv2,dk2=part(last,length,False)
            dv=dv+dv2; dk=dk+dk2
        for idx,val in ((1,dk*scale),(2,dv)):
            out=pl.ds(idx*columns+col,LANES)
            g_ref[first:last,out]=jnp.where(sel_b,val.astype(bf16),g_ref[first:last,out])
    out=pl.ds(col,LANES)
    g_ref[:,out]=jnp.where(sel,(dq[...]*scale).astype(bf16),g_ref[:,out])

def attn_bwd(count, qkv, do, o, lse, block=256):
    length,three=qkv.shape; columns=three//3; heads=columns//HD
    whole=lambda *s: pl.BlockSpec(s,lambda h:(0,)*len(s))
    return pl.pallas_call(
        functools.partial(attn_bwd_kernel,length=length,columns=columns,block=block),
        grid=(heads,),
        out_shape=jax.ShapeDtypeStruct((length,three),bf16),
        in_specs=[pl.BlockSpec(memory_space=pltpu.SMEM),whole(length,three),whole(length,columns),whole(length,columns),whole(heads,length)],
        out_specs=whole(length,three),
        scratch_shapes=[pltpu.VMEM((length,LANES),bf16)]*3+[pltpu.VMEM((length,LANES),f32)],
        compiler_params=pltpu.CompilerParams(vmem_limit_bytes=50<<20),
        cost_estimate=pl.CostEstimate(flops=10*length*length*columns,bytes_accessed=2*length*columns*8,transcendentals=length*length*heads//2),
        name="attn_bwd",
    )(count,qkv,do,o,lse)


def on_device(tokens, counts, gain_attn, gain_ffn, w_qkv, w_out, w_gate_up, w_down, cotangent):
    width = tokens.shape[1]
    columns = w_qkv.shape[2]
    hidden_cols = w_gate_up.shape[2]
    inputs = tokens.astype(jnp.float32)
    qkv_flat = w_qkv.reshape(width, 3 * columns)
    gate_up_flat = w_gate_up.reshape(width, 2 * hidden_cols)
    normed_attn = lax.all_gather(
        rms_scale(inputs, gain_attn).astype(jnp.bfloat16), "mp", axis=0, tiled=True
    )
    length = normed_attn.shape[0]
    projected = jnp.dot(normed_attn, qkv_flat, preferred_element_type=jnp.float32).astype(
        jnp.bfloat16
    )
    attended, log_totals = attn_fwd(counts, projected)
    piece = attended
    middle = inputs + lax.psum_scatter(
        jnp.dot(piece, w_out, preferred_element_type=jnp.float32),
        "mp",
        scatter_dimension=0,
        tiled=True,
    )
    normed_ffn = lax.all_gather(
        rms_scale(middle, gain_ffn).astype(jnp.bfloat16), "mp", axis=0, tiled=True
    )
    both = jnp.dot(normed_ffn, gate_up_flat, preferred_element_type=jnp.float32)
    gate = both[:, :hidden_cols]
    up = both[:, hidden_cols:]
    hidden = (jax.nn.silu(gate) * up).astype(jnp.bfloat16)
    piece = hidden
    latents = middle + lax.psum_scatter(
        jnp.dot(piece, w_down, preferred_element_type=jnp.float32).astype(jnp.bfloat16),
        "mp",
        scatter_dimension=0,
        tiled=True,
    ).astype(jnp.float32)
    upstream = cotangent.astype(jnp.float32)
    upstream_all = lax.all_gather(cotangent, "mp", axis=0, tiled=True)
    grad_w_down = jnp.einsum("rf,rd->fd", hidden, upstream_all, preferred_element_type=jnp.float32)
    grad_hidden = jnp.einsum("rd,fd->rf", upstream_all, w_down, preferred_element_type=jnp.float32)

    def swiglu(gate_in, up_in):
        return jax.nn.silu(gate_in) * up_in

    unused, swiglu_pull = jax.vjp(swiglu, gate, up)
    grad_gate, grad_up = swiglu_pull(grad_hidden)
    grad_both = jnp.concatenate([grad_gate, grad_up], axis=1).astype(jnp.bfloat16)
    grad_w_gate_up = jnp.einsum(
        "rd,rc->dc", normed_ffn, grad_both, preferred_element_type=jnp.float32
    ).reshape(width, 2, hidden_cols)
    piece = grad_both
    grad_normed_ffn = lax.psum_scatter(
        jnp.einsum("rc,dc->rd", piece, gate_up_flat, preferred_element_type=jnp.float32).astype(
            jnp.bfloat16
        ),
        "mp",
        scatter_dimension=0,
        tiled=True,
    ).astype(jnp.float32)
    unused, norm_pull = jax.vjp(rms_scale, middle, gain_ffn)
    grad_middle_norm, grad_gain_ffn = norm_pull(grad_normed_ffn)
    grad_middle = upstream + grad_middle_norm
    branch_grad = lax.all_gather(grad_middle.astype(jnp.bfloat16), "mp", axis=0, tiled=True)
    grad_w_out = jnp.einsum("rc,rd->cd", attended, branch_grad, preferred_element_type=jnp.float32)
    grad_attended = jnp.einsum("rd,cd->rc", branch_grad, w_out, preferred_element_type=jnp.float32)
    grad_projected = attn_bwd(
        counts, projected, grad_attended.astype(jnp.bfloat16), attended, log_totals
    )
    grad_w_qkv = jnp.einsum(
        "rd,rc->dc", normed_attn, grad_projected, preferred_element_type=jnp.float32
    ).reshape(width, 3, columns)
    piece = grad_projected
    grad_normed_attn = lax.psum_scatter(
        jnp.einsum("rc,dc->rd", piece, qkv_flat, preferred_element_type=jnp.float32).astype(
            jnp.bfloat16
        ),
        "mp",
        scatter_dimension=0,
        tiled=True,
    ).astype(jnp.float32)
    unused, first_pull = jax.vjp(rms_scale, inputs, gain_attn)
    grad_input_norm, grad_gain_attn = first_pull(grad_normed_attn)
    grad_tokens = grad_middle + grad_input_norm
    grad_w_qkv, grad_w_out, grad_w_gate_up, grad_w_down = [
        lax.psum(grad.astype(jnp.bfloat16), "dp").astype(jnp.float32)
        for grad in (grad_w_qkv, grad_w_out, grad_w_gate_up, grad_w_down)
    ]
    grad_gain_attn, grad_gain_ffn = lax.psum((grad_gain_attn, grad_gain_ffn), ("dp", "mp"))
    return (
        latents,
        grad_tokens,
        grad_gain_attn,
        grad_gain_ffn,
        grad_w_qkv,
        grad_w_out,
        grad_w_gate_up,
        grad_w_down,
    )


def solution(mesh):
    placed = (
        P(("dp", "mp"), None),
        P("dp"),
        P(),
        P(),
        P(None, None, "mp"),
        P("mp", None),
        P(None, None, "mp"),
        P("mp", None),
        P(("dp", "mp"), None),
    )
    return jax.shard_map(
        on_device,
        mesh=mesh,
        in_specs=placed,
        out_specs=(
            P(("dp", "mp"), None),
            P(("dp", "mp"), None),
            P(),
            P(),
            P(None, None, "mp"),
            P("mp", None),
            P(None, None, "mp"),
            P("mp", None),
        ),
        check_vma=False,
    )
```

time: 997 us -> 722 us (0.72)
  waiting for transfers between devices: 664 us -> 465 us
  matrix products: 179 us -> 87.6 us
  Pallas kernels: 0 us -> 58.1 us
  other arithmetic: 63.2 us -> 30.9 us
  local copies, waits for them, and re-layouts: 26.1 us -> 15.8 us
    psum x1, waiting for transfers between devices: 409 us -> 202 us  [on_device(): lax.psum(grad.astype(jnp.bfloat16), 'dp').astype(jnp.float32)]
    dot_general x24 -> x0, matrix products: 95.1 us -> none  [the longest x4 26.1 us: attend_backward(): jnp.einsum('qhd,khd->hqk', out_block, values[:last], preferred_element_ty...]
    pallas_call x0 -> x2, Pallas kernels: none -> 58.1 us  [the longest x1 36 us: attn_bwd(): pl.pallas_call(functools.partial(attn_bwd_kernel, length=length, columns=...]
    reduce_scatter x1, waiting for transfers between devices: 9.51 us -> 34.1 us  [on_device(): lax.psum_scatter(jnp.einsum('rc,dc->rd', piece, qkv_flat, preferred_eleme...]
    all_gather x1, waiting for transfers between devices: 34.3 us -> 13.5 us  [on_device(): lax.all_gather(grad_middle.astype(jnp.bfloat16), 'mp', axis=0, tiled=True)]
    convert_element_type x5 -> x4, other arithmetic: 26.5 us -> 11.1 us  [on_device(): lax.psum(grad.astype(jnp.bfloat16), 'dp').astype(jnp.float32)]
    unnamed x103 -> x37, local copies, waits for them, and re-layouts: 25.6 us -> 11.2 us
    reduce_sum x4 -> x0, other arithmetic: 12.4 us -> none  [attend_forward(): total = jnp.sum(expo, axis=-1, keepdims=True)]
  transfers between devices with their start and end apart: 9 -> 9, of which waited for: 9 -> 9; matrix products, arithmetic and copies ran while one was open for 6% -> 9% of each run, Pallas kernels for 0% -> 0%
where the time goes in v1:
time: 722 us; the launch traced here: 714 us
  waiting for transfers between devices  465 us (64%)
  matrix products  87.6 us (12%)
  Pallas kernels  58.1 us (8%)
  blocking collectives  39.7 us (5%)
  other arithmetic  30.9 us (4%)
  local copies, waits for them, and re-layouts  15.8 us (2%)
  between operations  14.8 us (2%)
    psum x1, waiting for transfers between devices, on_device(): lax.psum(grad.astype(jnp.bfloat16), 'dp').astype(jnp.float32)  202 us
    reduce_scatter x1, waiting for transfers between devices, on_device(): lax.psum_scatter(jnp.dot(piece, w_out, preferred_element_type=jnp.float32...  71.8 us
    reduce_scatter x1, waiting for transfers between devices, on_device(): lax.psum_scatter(jnp.einsum('rc,dc->rd', piece, gate_up_flat, preferred_e...  44.6 us
    psum x1, blocking collectives, on_device(): lax.psum((grad_gain_attn, grad_gain_ffn), ('dp', 'mp'))  39.7 us
    pallas_call x1, Pallas kernels, attn_bwd(): pl.pallas_call(functools.partial(attn_bwd_kernel, length=length, columns=...  36 us
    reduce_scatter x1, waiting for transfers between devices, on_device(): lax.psum_scatter(jnp.einsum('rc,dc->rd', piece, qkv_flat, preferred_eleme...  34.1 us
    all_gather x1, waiting for transfers between devices, on_device(): lax.all_gather(rms_scale(inputs, gain_attn).astype(jnp.bfloat16), 'mp', a...  34.1 us
    all_gather x1, waiting for transfers between devices, on_device(): lax.all_gather(rms_scale(middle, gain_ffn).astype(jnp.bfloat16), 'mp', ax...  33.7 us
  transfers between devices with their start and end apart: 9, of which 9 were waited for; matrix products, arithmetic and copies ran while one was open for 9% of the time, Pallas kernels for 0%

profile of v1, /device:TPU:0, one launch (start us, length us, event | category | flops | bytes accessed | tf_op | source)
XLA Modules:
  0.0 713.6 jit_solution(4218981925667165974)
XLA Ops:
  14.7 34.1 %all-gather.5.cloned.1.call-done = bf16[2048,1024]{1,0:T(8,128)(2,1)} async-done(((bf16[512,1024]{1,0:T(8,128)(2,1)}), bf16[2048,1024]{1,0:T(8,128)(2,1)}) %all-gather.5.cloned.1.call-update) | async-done | bytes 4194320 | tf_op jit(solution)/shard_map/all_gather | solution.py:160
  48.8 7.8 %convolution_convert_fusion.4.qkv_ref = bf16[2048,768]{1,0:T(8,128)(2,1)} fusion(bf16[2048,1024]{1,0:T(8,128)(2,1)} %all-gather.5.cloned.1.call-done, bf16[1024,768]{0,1:T(8,128)(2,1)} %bitcast.29), kind=kOutput, calls=%fused_computation.18 | convolution fusion | flops 3222798336 | bytes 8912896 | tf_op jit(solution)/shard_map/dot_general | solution.py:164
  56.6 22.1 %attn_fwd.1 = (bf16[2048,256]{1,0:T(8,128)(2,1)S(1)}, f32[4,2048]{1,0:T(4,128)S(1)}) custom-call(s32[1]{0:T(128)S(6)} %copy.26.count_ref, bf16[2048,768]{1,0:T(8,128)(2,1)} %convolution_convert_fusion.4.qkv_ref), custom_call_target="tpu_custom_call" | custom-call | flops 4294967296 | bytes 4194304 | tf_op jit(solution)/shard_map/attn_fwd/pallas_call | solution.py:75
  78.7 4.5 fusion.21
  84.3 71.8 %reduce-scatter.5.cloned.1.call-done = f32[512,1024]{1,0:T(8,128)} async-done(((f32[2048,1024]{1,0:T(8,128)}), f32[512,1024]{1,0:T(8,128)}) %reduce-scatter.5.cloned.1.call-update) | async-done | bytes 2097168 | tf_op jit(solution)/shard_map/reduce_scatter | solution.py:169
  161.8 33.7 %all-gather.7.cloned.1.call-done = bf16[2048,1024]{1,0:T(8,128)(2,1)} async-done(((bf16[512,1024]{1,0:T(8,128)(2,1)}), bf16[2048,1024]{1,0:T(8,128)(2,1)}) %all-gather.7.cloned.1.call-update) | async-done | bytes 4194320 | tf_op jit(solution)/shard_map/all_gather | solution.py:175
  195.5 11.3 %fusion.22 = f32[2048,1408]{0,1:T(8,128)} fusion(bf16[2048,1024]{1,0:T(8,128)(2,1)} %all-gather.7.cloned.1.call-done, bf16[1024,1408]{0,1:T(8,128)(2,1)S(1)} %bitcast.26), kind=kOutput, calls=%fused_computation.54 | convolution fusion | flops 5905580032 | bytes 18612224 | tf_op jit(solution)/shard_map/dot_general | solution.py:178
  206.8 24.7 %all-gather.9.cloned.1.call-done = bf16[2048,1024]{1,0:T(8,128)(2,1)} async-done(((bf16[512,1024]{1,0:T(8,128)(2,1)}), bf16[2048,1024]{1,0:T(8,128)(2,1)}) %all-gather.9.cloned.1.call-update) | async-done | bytes 4194320 | tf_op jit(solution)/shard_map/all_gather | solution.py:190
  231.5 11.1 %fusion.2 = (bf16[2048,704]{0,1:T(8,128)(2,1)S(1)}, bf16[2048,704]{0,1:T(8,128)(2,1)S(1)}, bf16[2048,704]{0,1:T(8,128)(2,1)}) fusion(f32[2048,1408]{0,1:T(8,128)} %fusion.22, bf16[2048,1024]{1,0:T(8,128)(2,1)} %all-gather.9.cloned.1.call-done, bf16[704,1024]{1,0:T(8,128)(2,1)} %param.16), kind=kOutput, calls=%fused_computation.3 | convolution fusion | flops 2975858688 | bytes 25821184 | tf_op jit(solution)/shard_map/rd,fd->rf/dot_general | solution.py:192
  245.1 8.3 %convolution_convert_fusion.1 = bf16[2048,1024]{1,0:T(8,128)(2,1)} fusion(bf16[1024,1408]{0,1:T(8,128)(2,1)S(1)} %bitcast.27, bf16[2048,704]{0,1:T(8,128)(2,1)S(1)} %get-tuple-element.25, bf16[2048,704]{0,1:T(8,128)(2,1)S(1)} %get-tuple-element.24), kind=kOutput, calls=%fused_computation.15 | convolution fusion | flops 5919211520 | bytes 12845056 | tf_op jit(solution)/shard_map/rc,dc->rd/dot_general | solution.py:205
  253.5 44.6 %reduce-scatter.9.cloned.1.call-done = bf16[512,1024]{1,0:T(8,128)(2,1)} async-done(((bf16[2048,1024]{1,0:T(8,128)(2,1)}), bf16[512,1024]{1,0:T(8,128)(2,1)}) %reduce-scatter.9.cloned.1.call-update) | async-done | bytes 1048592 | tf_op jit(solution)/shard_map/reduce_scatter | solution.py:204
  303.6 10.3 %convolution_convert_fusion = bf16[1024,1408]{1,0:T(8,128)(2,1)S(1)} fusion(bf16[2048,1024]{1,0:T(8,128)(2,1)} %all-gather.7.cloned.1.call-done, bf16[2048,704]{0,1:T(8,128)(2,1)} %copy-done.17, bf16[2048,704]{0,1:T(8,128)(2,1)} %copy-done.16), kind=kOutput, calls=%fused_computation.14 | convolution fusion | flops 5918556160 | bytes 12845056 | tf_op jit(solution)/shard_map/rd,rc->dc/dot_general | solution.py:200
  316.8 7.4 %convolution_convert_fusion.7 = bf16[704,1024]{1,0:T(8,128)(2,1)} fusion(bf16[2048,704]{0,1:T(8,128)(2,1)} %get-tuple-element.26, bf16[2048,1024]{1,0:T(8,128)(2,1)} %all-gather.9.cloned.1.call-done), kind=kOutput, calls=%fused_computation.42 | convolution fusion | flops 2953510912 | bytes 8519680 | tf_op jit(solution)/shard_map/rf,rd->fd/dot_general | solution.py:191
  324.2 13.5 %all-gather.11.cloned.1.call-done = bf16[2048,1024]{1,0:T(8,128)(2,1)} async-done(((bf16[512,1024]{1,0:T(8,128)(2,1)}), bf16[2048,1024]{1,0:T(8,128)(2,1)}) %all-gather.11.cloned.1.call-update) | async-done | bytes 4194320 | tf_op jit(solution)/shard_map/all_gather | solution.py:215
  341.2 36.0 %attn_bwd.1 = bf16[2048,768]{1,0:T(8,128)(2,1)} custom-call(s32[1]{0:T(128)S(6)} %copy.26.count_ref, bf16[2048,768]{1,0:T(8,128)(2,1)} %convolution_convert_fusion.4.qkv_ref, bf16[2048,256]{1,0:T(8,128)(2,1)S(1)} %convolution_convert_fusion.5.do_ref, bf16[2048,256]{1,0:T(8,128)(2,1)S(1)} %copy-done.3, f32[4,2048]{1,0:T(4,128)S(1)} %get-tuple-element.11.lse_ref), custom_call_target="tpu_custom_call" | custom-call | flops 10737418240 | bytes 8388608 | tf_op jit(solution)/shard_map/attn_bwd/pallas_call | solution.py:140
  377.2 5.4 convolution_convert_fusion.6
  384.3 4.3 convolution_convert_fusion.8
  390.0 6.9 convolution_convert_fusion.3
  398.3 6.9 convolution_convert_fusion.2
  405.3 202.4 %all-reduce.4.cloned.1.call-done = (bf16[1024,3,256]{2,0,1:T(8,128)(2,1)}, bf16[256,1024]{1,0:T(8,128)(2,1)}, bf16[1024,2,704]{0,2,1:T(8,128)(2,1)}, bf16[704,1024]{1,0:T(8,128)(2,1)}) async-done(((bf16[1024,3,256]{2,0,1:T(8,128)(2,1)}, bf16[256,1024]{1,0:T(8,128)(2,1)}, bf16[1024,2,704]{0,2,1:T(8,128)(2,1)}, bf16[704,1024]{1,0:T(8,128)(2,1)}), (bf16[1024,3,256]{2,0,1:T(8,128)(2,1)}, ...) | async-done | bytes 6422544 | tf_op jit(solution)/shard_map/psum | solution.py:237
  619.8 34.1 %reduce-scatter.11.cloned.1.call-done = bf16[512,1024]{1,0:T(8,128)(2,1)} async-done(((bf16[2048,1024]{1,0:T(8,128)(2,1)}), bf16[512,1024]{1,0:T(8,128)(2,1)}) %reduce-scatter.11.cloned.1.call-update) | async-done | bytes 1048592 | tf_op jit(solution)/shard_map/reduce_scatter | solution.py:225
  656.0 39.7 %all-reduce = (f32[1024]{0:T(1024)}, f32[1024]{0:T(1024)}) all-reduce(f32[1024]{0:T(1024)S(1)} %get-tuple-element.14, f32[1024]{0:T(1024)S(1)} %get-tuple-element.12), channel_id=1, replica_groups=mesh['dp'=8,'mp'=4] {'dp','mp'}, use_global_device_ids=true, to_apply=%region_9.10 | all-reduce | flops 2048 | bytes 16384 | tf_op jit(solution)/shard_map/psum | solution.py:240
  695.7 5.9 reduce-scatter.7.cloned.1.call-done
  701.7 5.2 fusion.13
  (73 shorter events, 46.8 us)
Async XLA Ops:
  7.2 188.4 %copy-start = (bf16[1024,2,704]{0,2,1:T(8,128)(2,1)S(1)}, bf16[1024,2,704]{0,2,1:T(8,128)(2,1)}, u32[]{:S(2)}) copy-start(bf16[1024,2,704]{0,2,1:T(8,128)(2,1)} %param.15) | copy-start | bytes 8650756
  7.2 41.6 %all-gather.5.cloned.1.call-start = ((), (), s32[]{:S(2)}) async-start(), calls=%async_computation.4 | async-start | bytes 5242880 | tf_op jit(solution)/shard_map/all_gather | solution.py:160
  11.4 144.7 %reduce-scatter.5.cloned.1.call-start = ((), (), s32[]{:S(2)}) async-start(), calls=%async_computation.5 | async-start | bytes 10485760 | tf_op jit(solution)/shard_map/reduce_scatter | solution.py:169
  56.6 22.1 %copy-start.11 = (bf16[256,1024]{1,0:T(8,128)(2,1)S(1)}, bf16[256,1024]{1,0:T(8,128)(2,1)}, u32[]{:S(2)}) copy-start(bf16[256,1024]{1,0:T(8,128)(2,1)} %param.14) | copy-start | bytes 1572868
  84.3 75.4 %copy-start.12 = (f32[1024]{0:T(1024)S(1)}, f32[1024]{0:T(1024)}, u32[]{:S(2)}) copy-start(f32[1024]{0:T(1024)} %param.12) | copy-start | bytes 12292
  84.3 111.2 %all-gather.7.cloned.1.call-start = ((), (), s32[]{:S(2)}) async-start(), calls=%async_computation.6 | async-start | bytes 5242880 | tf_op jit(solution)/shard_map/all_gather | solution.py:175
  160.9 70.6 %all-gather.9.cloned.1.call-start = ((), (), s32[]{:S(2)}) async-start(), calls=%async_computation.8 | async-start | bytes 5242880 | tf_op jit(solution)/shard_map/all_gather | solution.py:190
  161.5 136.7 %reduce-scatter.9.cloned.1.call-start = ((), (), s32[]{:S(2)}) async-start(), calls=%async_computation.9 | async-start | bytes 5242880 | tf_op jit(solution)/shard_map/reduce_scatter | solution.py:204
  242.6 1.6 copy-start.16
  242.6 2.6 copy-start.17
  253.5 44.7 %copy-start.5 = (f32[512,1024]{1,0:T(8,128)S(1)}, f32[512,1024]{1,0:T(8,128)}, u32[]{:S(2)}) copy-start(f32[512,1024]{1,0:T(8,128)} %copy-done.4) | copy-start | bytes 6291460
  253.5 84.2 %all-gather.11.cloned.1.call-start = ((), (), s32[]{:S(2)}) async-start(), calls=%async_computation.10 | async-start | bytes 5242880 | tf_op jit(solution)/shard_map/all_gather | solution.py:215
  298.2 2.0 copy-start.7
  303.0 304.7 %all-reduce.4.cloned.1.call-start = ((), (), s32[]{:S(2)}) async-start(), calls=%async_computation.12 | async-start | bytes 12845056 | tf_op jit(solution)/shard_map/psum | solution.py:237
  324.2 17.0 %copy-start.3 = (bf16[2048,256]{1,0:T(8,128)(2,1)S(1)}, bf16[2048,256]{1,0:T(8,128)(2,1)}, u32[]{:S(2)}) copy-start(bf16[2048,256]{1,0:T(8,128)(2,1)} %copy-done.2) | copy-start | bytes 3145732
  341.2 36.1 %copy-start.14 = (bf16[2048,1024]{1,0:T(8,128)(2,1)S(1)}, bf16[2048,1024]{1,0:T(8,128)(2,1)}, u32[]{:S(2)}) copy-start(bf16[2048,1024]{1,0:T(8,128)(2,1)} %all-gather.5.cloned.1.call-done) | copy-start | bytes 12582916
  388.6 1.4 copy-start.9
  388.6 265.2 %reduce-scatter.11.cloned.1.call-start = ((), (), s32[]{:S(2)}) async-start(), calls=%async_computation.11 | async-start | bytes 5242880 | tf_op jit(solution)/shard_map/reduce_scatter | solution.py:225
  397.0 304.7 %reduce-scatter.7.cloned.1.call-start = ((), (), s32[]{:S(2)}) async-start(), calls=%async_computation.7 | async-start | bytes 5242880 | tf_op jit(solution)/shard_map/reduce_scatter | solution.py:183
  607.7 5.6 copy-start.10
  613.3 3.0 copy-start.8
  616.2 37.6 %copy-start.6 = (bf16[512,1024]{1,0:T(8,128)(2,1)S(1)}, bf16[512,1024]{1,0:T(8,128)(2,1)}, u32[]{:S(2)}) copy-start(bf16[512,1024]{1,0:T(8,128)(2,1)} %param.9) | copy-start | bytes 3145732
  616.2 37.6 %copy-start.13 = (f32[1024]{0:T(1024)S(1)}, f32[1024]{0:T(1024)}, u32[]{:S(2)}) copy-start(f32[1024]{0:T(1024)} %param.11) | copy-start | bytes 12292
  701.7 5.2 copy-start.1
  (3 other events, 3.7 us)
Sparse Core Ops, SparseCore 0:
  11.5 37.1 all-gather.4
  84.4 71.6 reduce-scatter.4
  161.0 34.4 all-gather.6
  197.0 34.4 all-gather.8
  253.6 44.5 reduce-scatter.8
  303.2 34.4 all-gather.10
  388.8 218.8 all-reduce.3
  610.4 43.4 reduce-scatter.10
  656.4 45.2 reduce-scatter.6

commit v2 on v0

v2 whole, which is shorter than its diff:
```python
import functools

import jax
import jax.numpy as jnp
from jax import lax
from jax.experimental import pallas as pl
from jax.experimental.pallas import tpu as pltpu
from jax.sharding import PartitionSpec as P

HD = 64
EPS = 1e-05
LANES = 128
LOG2E = 1.4426950408889634
NN = (((1,), (0,)), ((), ()))
NT = (((1,), (1,)), ((), ()))
TN = (((0,), (0,)), ((), ()))
f32 = jnp.float32
bf16 = jnp.bfloat16
VMEM_LIMIT = 56 << 20


def dot(a, b, dims=NN):
    return lax.dot_general(a, b, dims, preferred_element_type=f32)


def whole(*shape):
    return pl.BlockSpec(shape, lambda *_: (0,) * len(shape))


def smem():
    return pl.BlockSpec(memory_space=pltpu.SMEM)


def shaped(shape, dtype):
    return jax.ShapeDtypeStruct(shape, dtype)


def params():
    return pltpu.CompilerParams(vmem_limit_bytes=VMEM_LIMIT)


def cost(flops, bytes_accessed, transcendentals=0):
    return pl.CostEstimate(
        flops=int(flops), bytes_accessed=int(bytes_accessed), transcendentals=int(transcendentals)
    )


def swap(value, bit, axis="mp"):
    size = lax.axis_size(axis)
    return lax.ppermute(value, axis, [(i, i ^ bit) for i in range(size)])


def after(value, *others):
    return lax.optimization_barrier((value,) + others)[0]


def gather_rel(value):
    far = swap(value, 2)
    near = swap(value, 1)
    return [value, near, far, swap(far, 1)]


def exchange_rel(parts):
    return [parts[0]] + [swap(parts[k], k) for k in (1, 2, 3)]


def add_low(a, b):
    return (a.astype(f32) + b.astype(f32)).astype(bf16)


def scatter_rel(parts):
    far = swap(add_low(parts[2], swap(parts[3], 1)), 2)
    return parts[0], swap(parts[1], 1), far


def head_lanes(rows, parity):
    lane = lax.broadcasted_iota(jnp.int32, (rows, LANES), 1)
    return (lane // HD) == parity, lane == (1 - parity) * HD


def project_kernel(a_ref, b_ref, w_ref, oa_ref, ob_ref):
    oa_ref[...] = dot(a_ref[...], w_ref[...]).astype(bf16)
    ob_ref[...] = dot(b_ref[...], w_ref[...]).astype(bf16)


def project(a, b, w):
    rows, width = a.shape
    out = w.shape[1]
    step = 256
    block = pl.BlockSpec((step, width), lambda i: (i, 0))
    block_out = pl.BlockSpec((step, out), lambda i: (i, 0))
    return pl.pallas_call(
        project_kernel,
        grid=(rows // step,),
        in_specs=[block, block, whole(width, out)],
        out_specs=[block_out, block_out],
        out_shape=[shaped((rows, out), bf16)] * 2,
        compiler_params=params(),
        cost_estimate=cost(4 * rows * width * out, 4 * rows * (width + out)),
        name="project",
    )(a, b, w)


def attn_fwd_kernel(me_ref, count_ref, p0_ref, p1_ref, n2_ref, n3_ref, w_ref, qkv_ref, o_ref, lse_ref, a0_ref, a1_ref, a2_ref, a3_ref, kaug, *, length, columns, block):
    h = pl.program_id(0)
    rows_each = length // 4
    me = me_ref[0]

    def spot(k):
        return pl.ds(pl.multiple_of((me ^ k) * rows_each, rows_each), rows_each)

    @pl.when(h == 0)
    def _():
        qkv_ref[spot(0), :] = p0_ref[...]
        qkv_ref[spot(1), :] = p1_ref[...]
        qkv_ref[spot(2), :] = dot(n2_ref[...], w_ref[...]).astype(bf16)
        qkv_ref[spot(3), :] = dot(n3_ref[...], w_ref[...]).astype(bf16)

    parity = lax.rem(h, 2)
    col = pl.multiple_of((h // 2) * LANES, LANES)
    c = HD**-0.5 * LOG2E
    sel, spare = head_lanes(length, parity)
    row = lax.broadcasted_iota(jnp.int32, (length, LANES), 0)
    k = qkv_ref[:, pl.ds(columns + col, LANES)].astype(f32)
    bias = jnp.where(row < count_ref[0], 0.0, -1e30)
    kaug[...] = jnp.where(sel, k, jnp.where(spare, bias, 0.0)).astype(bf16)
    sel_b, spare_b = head_lanes(block, parity)
    ri = lax.broadcasted_iota(jnp.int32, (block, block), 0)
    ci = lax.broadcasted_iota(jnp.int32, (block, block), 1)
    for i in range(length // block):
        first = i * block
        n = first + block
        rows = pl.ds(first, block)
        q = qkv_ref[rows, pl.ds(col, LANES)].astype(f32)
        q = jnp.where(sel_b, q, jnp.where(spare_b, 1.0, 0.0)).astype(bf16)
        s_d = dot(q, kaug[first:n], NT)
        s_d = jnp.where(ci <= ri, s_d, -1e30)
        m = jnp.max(s_d, axis=1, keepdims=True)
        if first:
            s_o = dot(q, kaug[:first], NT)
            m = jnp.maximum(m, jnp.max(s_o, axis=1, keepdims=True))
        mc = m * c
        p_d = jnp.exp2(s_d * c - mc)
        total = jnp.sum(p_d, axis=1, keepdims=True)
        o = dot(p_d.astype(bf16), qkv_ref[first:n, pl.ds(2 * columns + col, LANES)])
        if first:
            p_o = jnp.exp2(s_o * c - mc)
            total = total + jnp.sum(p_o, axis=1, keepdims=True)
            o = o + dot(p_o.astype(bf16), qkv_ref[:first, pl.ds(2 * columns + col, LANES)])
        o = (o / total).astype(bf16)
        out = pl.ds(col, LANES)
        o_ref[rows, out] = jnp.where(sel_b, o, o_ref[rows, out])
        lse = mc + jnp.log2(total)
        lse_ref[pl.ds(h, 1), first:n] = jnp.transpose(jnp.broadcast_to(lse, (block, LANES)))[0:1]

    @pl.when(h == pl.num_programs(0) - 1)
    def _():
        for k, ref in enumerate((a0_ref, a1_ref, a2_ref, a3_ref)):
            ref[...] = o_ref[spot(k), :]


def attn_fwd(me, count, p0, p1, n2, n3, w, block=256):
    each, width = n2.shape
    length = 4 * each
    three = w.shape[1]
    columns = three // 3
    heads = columns // HD
    return pl.pallas_call(
        functools.partial(attn_fwd_kernel, length=length, columns=columns, block=block),
        grid=(heads,),
        out_shape=[shaped((length, three), bf16), shaped((length, columns), bf16), shaped((heads, length), f32)]
        + [shaped((each, columns), bf16)] * 4,
        in_specs=[smem(), smem(), whole(each, three), whole(each, three), whole(each, width), whole(each, width), whole(width, three)],
        out_specs=[whole(length, three), whole(length, columns), whole(heads, length)] + [whole(each, columns)] * 4,
        scratch_shapes=[pltpu.VMEM((length, LANES), bf16)],
        compiler_params=params(),
        cost_estimate=cost(10 * length * length * columns, 2 * length * columns * 8, length * length * heads // 2),
        name="attn_fwd",
    )(me, count, p0, p1, n2, n3, w)


def attn_bwd_kernel(me_ref, count_ref, qkv_ref, d0_ref, d1_ref, d2_ref, d3_ref, o_ref, lse_ref, g_ref, do_all, kaug, qaug, dom, dq, *, length, columns, block):
    h = pl.program_id(0)
    rows_each = length // 4
    me = me_ref[0]

    @pl.when(h == 0)
    def _():
        for k, ref in enumerate((d0_ref, d1_ref, d2_ref, d3_ref)):
            do_all[pl.ds(pl.multiple_of((me ^ k) * rows_each, rows_each), rows_each), :] = ref[...]

    parity = lax.rem(h, 2)
    col = pl.multiple_of((h // 2) * LANES, LANES)
    scale = HD**-0.5
    c = scale * LOG2E
    sel, spare = head_lanes(length, parity)
    row = lax.broadcasted_iota(jnp.int32, (length, LANES), 0)
    k = qkv_ref[:, pl.ds(columns + col, LANES)].astype(f32)
    bias = jnp.where(row < count_ref[0], 0.0, -1e30)
    kaug[...] = jnp.where(sel, k, jnp.where(spare, bias, 0.0)).astype(bf16)
    q = qkv_ref[:, pl.ds(col, LANES)].astype(f32)
    qaug[...] = jnp.where(sel, q, jnp.where(spare, 1.0, 0.0)).astype(bf16)
    do = jnp.where(sel, do_all[:, pl.ds(col, LANES)].astype(f32), 0.0)
    dom[...] = do.astype(bf16)
    prod = do * o_ref[:, pl.ds(col, LANES)].astype(f32)
    hi = prod.astype(bf16)
    lo = (prod - hi.astype(f32)).astype(bf16)
    ones = jnp.ones((8, LANES), bf16)
    delta = (dot(ones, hi, NT) + dot(ones, lo, NT))[0:1]
    lse = lse_ref[pl.ds(h, 1), :]
    sel_b, _ = head_lanes(block, parity)
    ki = lax.broadcasted_iota(jnp.int32, (block, block), 0)
    qi = lax.broadcasted_iota(jnp.int32, (block, block), 1)
    dq[...] = jnp.zeros_like(dq)
    for j in range(length // block):
        first = j * block
        last = first + block
        kj = kaug[first:last]
        vj = qkv_ref[first:last, pl.ds(2 * columns + col, LANES)]

        def part(a, b, diag):
            s = dot(kj, qaug[a:b], NT)
            if diag:
                s = jnp.where(ki <= qi, s, -1e30)
            p = jnp.exp2(s * c - lse[:, a:b])
            dp = dot(vj, dom[a:b], NT)
            ds = (p * (dp - delta[:, a:b])).astype(bf16)
            dv = dot(p.astype(bf16), dom[a:b])
            dk = dot(ds, qaug[a:b])
            dq[a:b] += dot(ds, kj, TN)
            return dv, dk

        dv, dk = part(first, last, True)
        if last < length:
            dv2, dk2 = part(last, length, False)
            dv = dv + dv2
            dk = dk + dk2
        for idx, val in ((1, dk * scale), (2, dv)):
            out = pl.ds(idx * columns + col, LANES)
            g_ref[first:last, out] = jnp.where(sel_b, val.astype(bf16), g_ref[first:last, out])
    out = pl.ds(col, LANES)
    g_ref[:, out] = jnp.where(sel, (dq[...] * scale).astype(bf16), g_ref[:, out])


def attn_bwd(me, count, qkv, d_list, o, lse, block=256):
    length, three = qkv.shape
    columns = three // 3
    heads = columns // HD
    each = length // 4
    return pl.pallas_call(
        functools.partial(attn_bwd_kernel, length=length, columns=columns, block=block),
        grid=(heads,),
        out_shape=shaped((length, three), bf16),
        in_specs=[smem(), smem(), whole(length, three)] + [whole(each, columns)] * 4 + [whole(length, columns), whole(heads, length)],
        out_specs=whole(length, three),
        scratch_shapes=[pltpu.VMEM((length, columns), bf16)] + [pltpu.VMEM((length, LANES), bf16)] * 3 + [pltpu.VMEM((length, LANES), f32)],
        compiler_params=params(),
        cost_estimate=cost(20 * length * length * columns, 2 * length * columns * 8, length * length * heads // 2),
        name="attn_bwd",
    )(me, count, qkv, *d_list, o, lse)


def middle_kernel(x_ref, a0, a1, a2, a3, w0, w1, w2, w3, gain_ref, mid_ref, normed_ref):
    total = x_ref[...].astype(f32)
    acc = dot(a0[...], w0[...]) + dot(a1[...], w1[...]) + dot(a2[...], w2[...]) + dot(a3[...], w3[...])
    total = total + acc
    mid_ref[...] = total
    r = lax.rsqrt(jnp.mean(total * total, axis=1, keepdims=True) + EPS)
    normed_ref[...] = (total * r * gain_ref[...]).astype(bf16)


def middle_of(tokens, a_list, w_list, gain):
    rows, width = tokens.shape
    cols = a_list[0].shape[1]
    step = 128
    block = pl.BlockSpec((step, width), lambda i: (i, 0))
    block_a = pl.BlockSpec((step, cols), lambda i: (i, 0))
    return pl.pallas_call(
        middle_kernel,
        grid=(rows // step,),
        in_specs=[block] + [block_a] * 4 + [whole(cols, width)] * 4 + [whole(1, width)],
        out_specs=[block, block],
        out_shape=[shaped((rows, width), f32), shaped((rows, width), bf16)],
        compiler_params=params(),
        cost_estimate=cost(2 * rows * width * width, rows * width * 10 + 2 * width * width),
        name="middle",
    )(tokens, *a_list, *w_list, gain)


def ffn_kernel(na, nb, ca, cb, wg, wu, wd, hid_ref, gg_ref, gu_ref, pda, pdb, pga, pgb, xs, cs, *, half):
    i = pl.program_id(0)

    @pl.when(i < half)
    def _():
        xs[...] = na[...]
        cs[...] = ca[...]

    @pl.when(i >= half)
    def _():
        xs[...] = nb[...]
        cs[...] = cb[...]

    x = xs[...]
    gate = dot(x, wg[...])
    up = dot(x, wu[...])
    sig = jax.nn.sigmoid(gate)
    silu = gate * sig
    hidden = (silu * up).astype(bf16)
    hid_ref[...] = hidden
    grad_hidden = dot(cs[...], wd[...], NT)
    gg = (grad_hidden * up * sig * (1.0 + gate * (1.0 - sig))).astype(bf16)
    gu = (grad_hidden * silu).astype(bf16)
    gg_ref[...] = gg
    gu_ref[...] = gu
    down = dot(hidden, wd[...]).astype(bf16)
    grad_normed = (dot(gg, wg[...], NT) + dot(gu, wu[...], NT)).astype(bf16)

    @pl.when(i < half)
    def _():
        pda[...] = down
        pga[...] = grad_normed

    @pl.when(i >= half)
    def _():
        pdb[...] = down
        pgb[...] = grad_normed


def ffn(na, nb, ca, cb, wg, wu, wd):
    rows, width = na.shape
    hid = wg.shape[1]
    step = 256
    half = rows // step
    first = pl.BlockSpec((step, width), lambda i: (jnp.minimum(i, half - 1), 0))
    second = pl.BlockSpec((step, width), lambda i: (jnp.maximum(i - half, 0), 0))
    block_h = pl.BlockSpec((step, hid), lambda i: (i, 0))
    return pl.pallas_call(
        functools.partial(ffn_kernel, half=half),
        grid=(2 * half,),
        in_specs=[first, second, first, second, whole(width, hid), whole(width, hid), whole(hid, width)],
        out_specs=[block_h] * 3 + [first, second] * 2,
        out_shape=[shaped((2 * rows, hid), bf16)] * 3 + [shaped((rows, width), bf16)] * 4,
        scratch_shapes=[pltpu.VMEM((step, width), bf16)] * 2,
        compiler_params=params(),
        cost_estimate=cost(24 * rows * width * hid, 12 * rows * (width + hid), 2 * rows * hid),
        name="ffn",
    )(na, nb, ca, cb, wg, wu, wd)


def grad_middle_kernel(cot, mid, g0, g1, g2, gain, w0, w1, w2, w3, gm_ref, gml_ref, o0, o1, o2, o3, gg_ref):
    dn = g0[...].astype(f32) + g1[...].astype(f32) + g2[...].astype(f32)
    x = mid[...]
    r = lax.rsqrt(jnp.mean(x * x, axis=1, keepdims=True) + EPS)
    e = dn * gain[...]
    gm = cot[...].astype(f32) + r * e - x * (r * r * r * jnp.mean(e * x, axis=1, keepdims=True))
    gm_ref[...] = gm
    low = gm.astype(bf16)
    gml_ref[...] = low
    for w, o in ((w0, o0), (w1, o1), (w2, o2), (w3, o3)):
        o[...] = dot(low, w[...], NT).astype(bf16)
    part = jnp.sum(dn * x * r, axis=0, keepdims=True)

    @pl.when(pl.program_id(0) == 0)
    def _():
        gg_ref[...] = part

    @pl.when(pl.program_id(0) > 0)
    def _():
        gg_ref[...] += part


def grad_middle_of(cot, mid, parts, gain, w_list):
    rows, width = cot.shape
    cols = w_list[0].shape[0]
    step = 128
    block = pl.BlockSpec((step, width), lambda i: (i, 0))
    block_a = pl.BlockSpec((step, cols), lambda i: (i, 0))
    return pl.pallas_call(
        grad_middle_kernel,
        grid=(rows // step,),
        in_specs=[block] * 5 + [whole(1, width)] + [whole(cols, width)] * 4,
        out_specs=[block, block] + [block_a] * 4 + [whole(1, width)],
        out_shape=[shaped((rows, width), f32), shaped((rows, width), bf16)] + [shaped((rows, cols), bf16)] * 4 + [shaped((1, width), f32)],
        compiler_params=params(),
        cost_estimate=cost(2 * rows * width * width, rows * width * 20 + 2 * width * width),
        name="grad_middle",
    )(cot, mid, *parts, gain, *w_list)


def grad_tokens_kernel(gm, tok, g0, g1, g2, gain, out_ref, gg_ref):
    dn = g0[...].astype(f32) + g1[...].astype(f32) + g2[...].astype(f32)
    x = tok[...].astype(f32)
    r = lax.rsqrt(jnp.mean(x * x, axis=1, keepdims=True) + EPS)
    e = dn * gain[...]
    out_ref[...] = gm[...] + r * e - x * (r * r * r * jnp.mean(e * x, axis=1, keepdims=True))
    part = jnp.sum(dn * x * r, axis=0, keepdims=True)

    @pl.when(pl.program_id(0) == 0)
    def _():
        gg_ref[...] = part

    @pl.when(pl.program_id(0) > 0)
    def _():
        gg_ref[...] += part


def grad_tokens_of(gm, tokens, parts, gain):
    rows, width = gm.shape
    step = 128
    block = pl.BlockSpec((step, width), lambda i: (i, 0))
    return pl.pallas_call(
        grad_tokens_kernel,
        grid=(rows // step,),
        in_specs=[block] * 5 + [whole(1, width)],
        out_specs=[block, whole(1, width)],
        out_shape=[shaped((rows, width), f32), shaped((1, width), f32)],
        compiler_params=params(),
        cost_estimate=cost(rows * width * 20, rows * width * 20),
        name="grad_tokens",
    )(gm, tokens, *parts, gain)


def qkv_dgrad_kernel(me_ref, g_ref, w_ref, oa_ref, ob_ref, *, ka, kb):
    each = oa_ref.shape[0]
    me = me_ref[0]
    for k, o in ((ka, oa_ref), (kb, ob_ref)):
        rows = pl.ds(pl.multiple_of((me ^ k) * each, each), each)
        o[...] = dot(g_ref[rows, :], w_ref[...], NT).astype(bf16)


def qkv_dgrad(me, grad, w, ka, kb):
    length, three = grad.shape
    width = w.shape[0]
    each = length // 4
    return pl.pallas_call(
        functools.partial(qkv_dgrad_kernel, ka=ka, kb=kb),
        in_specs=[smem(), pl.BlockSpec(memory_space=pltpu.VMEM), pl.BlockSpec(memory_space=pltpu.VMEM)],
        out_specs=[pl.BlockSpec(memory_space=pltpu.VMEM)] * 2,
        out_shape=[shaped((each, width), bf16)] * 2,
        compiler_params=params(),
        cost_estimate=cost(4 * each * width * three, 2 * (length * three + width * three + 2 * each * width)),
        name="qkv_dgrad",
    )(me, grad, w)


def place(block, me):
    rel = block ^ me
    return (rel & 1) * 4 + ((rel >> 1) & 1) * 2 + (rel >> 2)


def unplace(position, me):
    rel = (position >> 2) | (((position >> 1) & 1) << 1) | ((position & 1) << 2)
    return rel ^ me


def wgrad_down_kernel(dp_ref, ha, hb, c0, c1, c2, c3, o_ref, acc, *, each):
    acc[...] = dot(ha[:each], c0[...], TN)
    acc[...] += dot(ha[each:], c1[...], TN)
    acc[...] += dot(hb[:each], c2[...], TN)
    acc[...] += dot(hb[each:], c3[...], TN)
    wide = o_ref.shape[2]
    for b in range(8):
        o_ref[place(b, dp_ref[0])] = acc[:, b * wide : (b + 1) * wide].astype(bf16)


def wgrad_down(dp, ha, hb, c_list):
    hid = ha.shape[1]
    each, width = c_list[0].shape
    vm = pl.BlockSpec(memory_space=pltpu.VMEM)
    return pl.pallas_call(
        functools.partial(wgrad_down_kernel, each=each),
        in_specs=[smem()] + [vm] * 6,
        out_specs=vm,
        out_shape=shaped((8, hid, width // 8), bf16),
        scratch_shapes=[pltpu.VMEM((hid, width), f32)],
        compiler_params=params(),
        cost_estimate=cost(8 * each * width * hid, 8 * each * (width + hid) + 2 * width * hid),
        name="wgrad_down",
    )(dp, ha, hb, *c_list)


def wgrad_gate_up_kernel(dp_ref, ga, gb, ua, ub, n0, n1, n2, n3, o_ref, acc, *, each):
    tall = o_ref.shape[2]
    for idx, (a, b) in enumerate(((ga, gb), (ua, ub))):
        acc[...] = dot(n0[...], a[:each], TN)
        acc[...] += dot(n1[...], a[each:], TN)
        acc[...] += dot(n2[...], b[:each], TN)
        acc[...] += dot(n3[...], b[each:], TN)
        for blk in range(8):
            o_ref[place(blk, dp_ref[0]), idx] = acc[blk * tall : (blk + 1) * tall].astype(bf16)


def wgrad_gate_up(dp, ga, gb, ua, ub, n_list):
    hid = ga.shape[1]
    each, width = n_list[0].shape
    vm = pl.BlockSpec(memory_space=pltpu.VMEM)
    return pl.pallas_call(
        functools.partial(wgrad_gate_up_kernel, each=each),
        in_specs=[smem()] + [vm] * 8,
        out_specs=vm,
        out_shape=shaped((8, 2, width // 8, hid), bf16),
        scratch_shapes=[pltpu.VMEM((width, hid), f32)],
        compiler_params=params(),
        cost_estimate=cost(16 * each * width * hid, 8 * each * (width + 2 * hid) + 4 * width * hid),
        name="wgrad_gate_up",
    )(dp, ga, gb, ua, ub, *n_list)


def wgrad_out_kernel(gml, a0, a1, a2, a3, o0, o1, o2, o3):
    for a, o in ((a0, o0), (a1, o1), (a2, o2), (a3, o3)):
        o[...] = dot(gml[...], a[...], TN).astype(bf16)


def wgrad_out(gml, a_list):
    each, width = gml.shape
    cols = a_list[0].shape[1]
    vm = pl.BlockSpec(memory_space=pltpu.VMEM)
    return pl.pallas_call(
        wgrad_out_kernel,
        in_specs=[vm] * 5,
        out_specs=[vm] * 4,
        out_shape=[shaped((width, cols), bf16)] * 4,
        compiler_params=params(),
        cost_estimate=cost(8 * each * width * cols, 4 * each * width + 2 * width * width),
        name="wgrad_out",
    )(gml, *a_list)


def wgrad_qkv_kernel(me_ref, dp_ref, g_ref, n0, n1, n2, n3, w0, w1, w2, o_ref, acc, *, each):
    me = me_ref[0]
    for k, n in enumerate((n0, n1, n2, n3)):
        rows = pl.ds(pl.multiple_of((me ^ k) * each, each), each)
        term = dot(n[...], g_ref[rows, :], TN)
        if k:
            acc[...] += term
        else:
            acc[...] = term
    tall = o_ref.shape[1]
    three = g_ref.shape[1]
    for blk in range(8):
        rows = slice(blk * tall, (blk + 1) * tall)
        spot = place(blk, dp_ref[0])
        o_ref[spot, :, :three] = acc[rows].astype(bf16)
        out = w0[rows].astype(f32) + w1[rows].astype(f32) + w2[rows].astype(f32)
        o_ref[spot, :, three:] = out.astype(bf16)


def wgrad_qkv(me, dp, grad, n_list, w_parts):
    length, three = grad.shape
    each, width = n_list[0].shape
    cols = w_parts[0].shape[1]
    vm = pl.BlockSpec(memory_space=pltpu.VMEM)
    return pl.pallas_call(
        functools.partial(wgrad_qkv_kernel, each=each),
        in_specs=[smem(), smem()] + [vm] * 8,
        out_specs=vm,
        out_shape=shaped((8, width // 8, three + cols), bf16),
        scratch_shapes=[pltpu.VMEM((width, three), f32)],
        compiler_params=params(),
        cost_estimate=cost(2 * length * width * three, 2 * length * (width + three) + 2 * width * (three + 4 * cols)),
        name="wgrad_qkv",
    )(me, dp, grad, *n_list, *w_parts)


def reduce_dp(value):
    if lax.axis_size("dp") != 8:
        total = lax.psum(value, "dp")
        return total[0:1], total[1:2], total[2:4], total[4:8]
    kept = value[:4]
    got = swap(value[4:], 1, "dp")
    kept, sent = add_low(kept[:2], got[:2]), add_low(kept[2:], got[2:])
    got = swap(sent, 2, "dp")
    kept, sent = add_low(kept[:1], got[:1]), add_low(kept[1:], got[1:])
    got = swap(sent, 4, "dp")
    own = add_low(kept, got)
    one = swap(own, 4, "dp")
    pair = jnp.concatenate([own, one], axis=0)
    two = swap(pair, 2, "dp")
    four = swap(jnp.concatenate([pair, two], axis=0), 1, "dp")
    return own, one, two, four


def pieces(refs):
    position = 0
    for ref in refs:
        for i in range(ref.shape[0]):
            yield position, ref, i
            position += 1


def finish_down_kernel(dp_ref, p0, p1, p2, p4, o_ref):
    wide = p0.shape[2]
    for position, ref, i in pieces((p0, p1, p2, p4)):
        b = unplace(position, dp_ref[0])
        o_ref[:, pl.ds(pl.multiple_of(b * wide, wide), wide)] = ref[i].astype(f32)


def finish_gate_up_kernel(dp_ref, p0, p1, p2, p4, o_ref):
    tall = p0.shape[2]
    for position, ref, i in pieces((p0, p1, p2, p4)):
        b = unplace(position, dp_ref[0])
        rows = pl.ds(pl.multiple_of(b * tall, tall), tall)
        for idx in range(2):
            o_ref[rows, idx, :] = ref[i, idx].astype(f32)


def finish_qkv_kernel(dp_ref, p0, p1, p2, p4, o_ref, out_ref):
    tall = p0.shape[1]
    cols = out_ref.shape[0]
    for position, ref, i in pieces((p0, p1, p2, p4)):
        b = unplace(position, dp_ref[0])
        rows = pl.ds(pl.multiple_of(b * tall, tall), tall)
        for idx in range(3):
            o_ref[rows, idx, :] = ref[i, :, idx * cols : (idx + 1) * cols].astype(f32)
        out_ref[:, rows] = jnp.transpose(ref[i, :, 3 * cols :].astype(f32))


def finish(kernel, dp, parts, shapes, name):
    vm = pl.BlockSpec(memory_space=pltpu.VMEM)
    return pl.pallas_call(
        kernel,
        in_specs=[smem()] + [vm] * 4,
        out_specs=[vm] * len(shapes),
        out_shape=[shaped(s, f32) for s in shapes],
        compiler_params=params(),
        cost_estimate=cost(1e6, 6 * sum(p.size for p in parts)),
        name=name,
    )(dp, *parts)


def sum_all(value):
    for axis in ("mp", "dp"):
        size = lax.axis_size(axis)
        bit = 1
        while bit < size:
            value = value + swap(value, bit, axis)
            bit *= 2
    return value


def rms_scale(values, gain):
    return values * lax.rsqrt(jnp.mean(values * values, axis=-1, keepdims=True) + EPS) * gain


def on_device(tokens, counts, gain_attn, gain_ffn, w_qkv, w_out, w_gate_up, w_down, cotangent):
    rows, width = tokens.shape
    columns = w_qkv.shape[2]
    hid = w_gate_up.shape[2]
    me = lax.axis_index("mp").astype(jnp.int32).reshape(1)
    dp = jnp.zeros((1,), jnp.int32)
    if lax.axis_size("dp") == 8:
        dp = lax.axis_index("dp").astype(jnp.int32).reshape(1)
    gain_a = gain_attn.reshape(1, width)
    gain_f = gain_ffn.reshape(1, width)
    qkv_w = w_qkv.reshape(width, 3 * columns)
    gate_w = w_gate_up[:, 0, :]
    up_w = w_gate_up[:, 1, :]

    normed = rms_scale(tokens.astype(f32), gain_attn).astype(bf16)
    n = gather_rel(normed)
    p0, p1 = project(n[0], n[1], qkv_w)
    out_w = gather_rel(after(w_out, n[2]))
    cot = gather_rel(after(cotangent, out_w[2]))
    qkv, attended, lse, *a = attn_fwd(me, counts, p0, p1, n[2], n[3], qkv_w)
    a = exchange_rel(a)
    middle, normed_ffn = middle_of(tokens, a, out_w, gain_f)
    m = gather_rel(normed_ffn)
    hid_a, gg_a, gu_a, d0, d1, g0, g1 = ffn(m[0], m[1], cot[0], cot[1], gate_w, up_w, w_down)
    hid_b, gg_b, gu_b, d2, d3, g2, g3 = ffn(m[2], m[3], cot[2], cot[3], gate_w, up_w, w_down)
    s = scatter_rel((g0, g1, g2, g3))
    down = wgrad_down(dp, hid_a, hid_b, cot)
    down = reduce_dp(down)
    gate_up = reduce_dp(wgrad_gate_up(dp, gg_a, gg_b, gu_a, gu_b, m))
    grad_middle, low, *ga, gain_f_part = grad_middle_of(cotangent, middle, s, gain_f, out_w)
    d_list = exchange_rel(ga)
    lat = scatter_rel([after(v, d_list[2], d_list[3]) for v in (d0, d1, d2, d3)])
    latents = middle + lat[0].astype(f32) + lat[1].astype(f32) + lat[2].astype(f32)
    w_parts = scatter_rel(wgrad_out(low, a))
    grad = attn_bwd(me, counts, qkv, d_list, attended, lse)
    t2, t3 = qkv_dgrad(me, grad, qkv_w, 2, 3)
    t0, t1 = qkv_dgrad(me, grad, qkv_w, 0, 1)
    t = scatter_rel((t0, t1, t2, t3))
    last = reduce_dp(wgrad_qkv(me, dp, grad, n, w_parts))
    grad_tokens, gain_a_part = grad_tokens_of(grad_middle, tokens, t, gain_a)
    gains = sum_all(jnp.concatenate([gain_a_part, gain_f_part], axis=0))
    (grad_w_down,) = finish(finish_down_kernel, dp, down, [(hid, width)], "finish_down")
    (grad_w_gate_up,) = finish(finish_gate_up_kernel, dp, gate_up, [(width, 2, hid)], "finish_gate_up")
    grad_w_qkv, grad_w_out = finish(finish_qkv_kernel, dp, last, [(width, 3, columns), (columns, width)], "finish_qkv")
    return (
        latents,
        grad_tokens,
        gains[0],
        gains[1],
        grad_w_qkv,
        grad_w_out,
        grad_w_gate_up,
        grad_w_down,
    )


def solution(mesh):
    placed = (
        P(("dp", "mp"), None),
        P("dp"),
        P(),
        P(),
        P(None, None, "mp"),
        P("mp", None),
        P(None, None, "mp"),
        P("mp", None),
        P(("dp", "mp"), None),
    )
    return jax.shard_map(
        on_device,
        mesh=mesh,
        in_specs=placed,
        out_specs=(
            P(("dp", "mp"), None),
            P(("dp", "mp"), None),
            P(),
            P(),
            P(None, None, "mp"),
            P("mp", None),
            P(None, None, "mp"),
            P("mp", None),
        ),
        check_vma=False,
    )
```

time: 997 us -> 510 us (0.51)
  waiting for transfers between devices: 664 us -> 191 us
  matrix products: 179 us -> 0 us
  Pallas kernels: 0 us -> 178 us
  starting transfers between devices: 0.72 us -> 50.4 us
  blocking collectives: 39.7 us -> 0 us
  other arithmetic: 63.2 us -> 33.3 us
  local copies, waits for them, and re-layouts: 26.1 us -> 46.3 us
  between operations: 15.4 us -> 1.97 us
    psum x1 -> x0, waiting for transfers between devices: 409 us -> none  [on_device(): lax.psum((grad_w_qkv, grad_w_out, grad_w_gate_up, grad_w_down), 'dp')]
    ppermute x0 -> x53, waiting for transfers between devices: none -> 191 us  [swap(): return lax.ppermute(value, axis, [(i, i ^ bit) for i in range(size)])]
    dot_general x36 -> x0, matrix products: 179 us -> none  [the longest x4 26.1 us: attend_backward(): jnp.einsum('qhd,khd->hqk', out_block, values[:last], preferred_element_ty...]
    pallas_call x0 -> x17, Pallas kernels: none -> 178 us  [the longest x1 36.9 us: attn_bwd(): pl.pallas_call(functools.partial(attn_bwd_kernel, length=length, columns=...]
    reduce_scatter x4 -> x0, waiting for transfers between devices: 132 us -> none  [the longest x1 71.8 us: on_device(): lax.psum_scatter(jnp.dot(piece, w_out, preferred_element_type=jnp.float32...]
    all_gather x4 -> x0, waiting for transfers between devices: 123 us -> none  [the longest x1 34.3 us: on_device(): lax.all_gather(grad_middle.astype(jnp.bfloat16), 'mp', axis=0, tiled=True)]
    ppermute x0 -> x53, starting transfers between devices: none -> 50.4 us  [swap(): return lax.ppermute(value, axis, [(i, i ^ bit) for i in range(size)])]
    psum x1 -> x0, blocking collectives: 39.7 us -> none  [on_device(): lax.psum((grad_gain_attn, grad_gain_ffn), ('dp', 'mp'))]
  transfers between devices with their start and end apart: 9 -> 53, of which waited for: 9 -> 20; matrix products, arithmetic and copies ran while one was open for 6% -> 13% of each run, Pallas kernels for 0% -> 29%
where the time goes in v2:
time: 510 us; the launch traced here: 501 us
  waiting for transfers between devices  191 us (37%)
  Pallas kernels  178 us (35%)
  starting transfers between devices  50.4 us (10%)
  local copies, waits for them, and re-layouts  46.3 us (9%)
  other arithmetic  33.3 us (7%)
    ppermute x53, waiting for transfers between devices, swap(): return lax.ppermute(value, axis, [(i, i ^ bit) for i in range(size)])  191 us
    ppermute x53, starting transfers between devices, swap(): return lax.ppermute(value, axis, [(i, i ^ bit) for i in range(size)])  50.4 us
    pallas_call x1, Pallas kernels, attn_bwd(): pl.pallas_call(functools.partial(attn_bwd_kernel, length=length, columns=...  36.9 us
    pallas_call x2, Pallas kernels, ffn(): pl.pallas_call(functools.partial(ffn_kernel, half=half), grid=(2 * half,)...  33.3 us
    pallas_call x1, Pallas kernels, attn_fwd(): pl.pallas_call(functools.partial(attn_fwd_kernel, length=length, columns=...  27.2 us
    unnamed x61, local copies, waits for them, and re-layouts  26.9 us
    convert_element_type x13, other arithmetic, add_low(): return (a.astype(f32) + b.astype(f32)).astype(bf16)  19.5 us
    pallas_call x3, Pallas kernels, finish(): pl.pallas_call(kernel, in_specs=[smem()] + [vm] * 4, out_specs=[vm] * len...  14.4 us
  transfers between devices with their start and end apart: 53, of which 20 were waited for; matrix products, arithmetic and copies ran while one was open for 13% of the time, Pallas kernels for 29%

profile of v2, /device:TPU:0, one launch (start us, length us, event | category | flops | bytes accessed | tf_op | source)
XLA Modules:
  0.0 500.9 jit_solution(2707454165092296784)
XLA Ops:
  7.7 23.5 %collective-permute-done.1.n2_ref.n2 = bf16[512,1024]{1,0:T(8,128)(2,1)} collective-permute-done((bf16[512,1024]{1,0:T(8,128)(2,1)}, bf16[512,1024]{1,0:T(8,128)(2,1)}, u32[]{:S(2)}, u32[]{:S(2)}) %collective-permute-start.1) | collective-permute-done | bytes 1048608 | tf_op jit(solution)/shard_map/ppermute | solution.py:50
  45.5 27.2 %attn_fwd.1 = (bf16[2048,768]{1,0:T(8,128)(2,1)}, bf16[2048,256]{1,0:T(8,128)(2,1)}, f32[4,2048]{1,0:T(4,128)}, bf16[512,256]{1,0:T(8,128)(2,1)}, bf16[512,256]{...) custom-call(s32[1]{0:T(128)} %bitcast.me_ref, s32[1]{0:T(128)S(6)} %copy.57.count_ref, ...), custom_call_target="tpu_custom_call" | custom-call | flops 10737418240 | bytes 8388608 | tf_op jit(solution)/shard_map/attn_fwd/pallas_call | solution.py:168
  76.3 6.1 %collective-permute-done.4.a2 = bf16[512,256]{1,0:T(8,128)(2,1)S(1)} collective-permute-done((bf16[512,256]{1,0:T(8,128)(2,1)}, bf16[512,256]{1,0:T(8,128)(2,1)S(1)}, u32[]{:S(2)}, u32[]{:S(2)}) %collective-permute-start.4) | collective-permute-done | bytes 262176 | tf_op jit(solution)/shard_map/ppermute | solution.py:50
  88.1 5.6 %middle.1 = (f32[512,1024]{1,0:T(8,128)}, bf16[512,1024]{1,0:T(8,128)(2,1)}) custom-call(bf16[512,1024]{1,0:T(8,128)(2,1)} %tok.1, bf16[512,256]{1,0:T(8,128)(2,1)} %get-tuple-element.60.a0, bf16[512,256]{1,0:T(8,128)(2,1)} %copy-done.19, bf16[512,256]{1,0:T(8,128)(2,1)} %copy-done.20, bf16[512,256]{1,0:T(8,128)(2,1)} %copy-done.21, bf16[256,1024]{1,0:T(8,128)(2,1)} %w0.1, ...), custom_call_target="tpu_custom_call" | custom-call | flops 1073741824 | bytes 7340032 | tf_op jit(solution)/shard_map/middle/pallas_call | solution.py:278
  95.5 15.0 %collective-permute-done.14.ca.c2 = bf16[512,1024]{1,0:T(8,128)(2,1)} collective-permute-done((bf16[512,1024]{1,0:T(8,128)(2,1)}, bf16[512,1024]{1,0:T(8,128)(2,1)}, u32[]{:S(2)}, u32[]{:S(2)}) %collective-permute-start.14) | collective-permute-done | bytes 1048608 | tf_op jit(solution)/shard_map/ppermute | solution.py:50
  110.6 21.7 %collective-permute-done.12.na.n2 = bf16[512,1024]{1,0:T(8,128)(2,1)} collective-permute-done((bf16[512,1024]{1,0:T(8,128)(2,1)}, bf16[512,1024]{1,0:T(8,128)(2,1)}, u32[]{:S(2)}, u32[]{:S(2)}) %collective-permute-start.12) | collective-permute-done | bytes 1048608 | tf_op jit(solution)/shard_map/ppermute | solution.py:50
  137.5 16.7 %ffn.2 = (bf16[1024,704]{1,0:T(8,128)(2,1)}, bf16[1024,704]{1,0:T(8,128)(2,1)}, bf16[1024,704]{1,0:T(8,128)(2,1)}, bf16[512,1024]{1,0:T(8,128)(2,1)}, bf16[512,1...) custom-call(bf16[512,1024]{1,0:T(8,128)(2,1)} %get-tuple-element.66.na.n0, ...), custom_call_target="tpu_custom_call" | custom-call | flops 8858370048 | bytes 10616832 | tf_op jit(solution)/shard_map/ffn/pallas_call | solution.py:337
  154.2 16.7 %ffn.3 = (bf16[1024,704]{1,0:T(8,128)(2,1)}, bf16[1024,704]{1,0:T(8,128)(2,1)}, bf16[1024,704]{1,0:T(8,128)(2,1)}, bf16[512,1024]{1,0:T(8,128)(2,1)}, bf16[512,1...) custom-call(bf16[512,1024]{1,0:T(8,128)(2,1)} %collective-permute-done.12.na.n2, ...), custom_call_target="tpu_custom_call" | custom-call | flops 8858370048 | bytes 10616832 | tf_op jit(solution)/shard_map/ffn/pallas_call | solution.py:337
  170.8 12.7 %wgrad_gate_up.1 = bf16[8,2,128,704]{3,2,1,0:T(8,128)(2,1)} custom-call(s32[1]{0:T(128)} %bitcast.8.dp_ref, bf16[1024,704]{1,0:T(8,128)(2,1)} %get-tuple-element.102.ga, bf16[1024,704]{1,0:T(8,128)(2,1)} %get-tuple-element.103.gb, bf16[1024,704]{1,0:T(8,128)(2,1)} %get-tuple-element.104.ua, bf16[1024,704]{1,0:T(8,128)(2,1)} %get-tuple-element.105.ub, ...), custom_call_target="tpu_custom_call" | custom-call | flops 5905580032 | bytes 12845056 | tf_op jit(solution)/shard_map/wgrad_gate_up/pallas_call | solution.py:497
  188.3 7.5 %wgrad_down.1 = bf16[8,704,128]{2,1,0:T(8,128)(2,1)} custom-call(s32[1]{0:T(128)} %bitcast.8.dp_ref, bf16[1024,704]{1,0:T(8,128)(2,1)} %get-tuple-element.106.ha, bf16[1024,704]{1,0:T(8,128)(2,1)} %get-tuple-element.107.hb, bf16[512,1024]{1,0:T(8,128)(2,1)} %c0, bf16[512,1024]{1,0:T(8,128)(2,1)} %collective-permute-done.10.cb.c1, ...), custom_call_target="tpu_custom_call" | custom-call | flops 2952790016 | bytes 8519680 | tf_op jit(solution)/shard_map/wgrad_down/pallas_call | solution.py:470
  201.3 19.1 %collective-permute-done.41 = bf16[4,2,128,704]{2,3,1,0:T(8,128)(2,1)S(1)} collective-permute-done((bf16[4,2,128,704]{2,3,1,0:T(8,128)(2,1)S(1)}, bf16[4,2,128,704]{2,3,1,0:T(8,128)(2,1)S(1)}, u32[]{:S(2)}, u32[]{:S(2)}) %collective-permute-start.41) | collective-permute-done | bytes 1441824 | tf_op jit(solution)/shard_map/ppermute | solution.py:50
  239.0 8.2 %grad_middle.1 = (f32[512,1024]{1,0:T(8,128)}, bf16[512,1024]{1,0:T(8,128)(2,1)}, bf16[512,256]{1,0:T(8,128)(2,1)}, bf16[512,256]{1,0:T(8,128)(2,1)}, bf16[512,2...) custom-call(bf16[512,1024]{1,0:T(8,128)(2,1)} %c0, f32[512,1024]{1,0:T(8,128)} %get-tuple-element.65.mid, ...), custom_call_target="tpu_custom_call" | custom-call | flops 1073741824 | bytes 12582912 | tf_op jit(solution)/shard_map/grad_middle/pallas_call | solution.py:378
  251.0 5.2 %collective-permute-done.48 = bf16[2,704,128]{2,1,0:T(8,128)(2,1)S(1)} collective-permute-done((bf16[2,704,128]{2,1,0:T(8,128)(2,1)S(1)}, bf16[2,704,128]{2,1,0:T(8,128)(2,1)S(1)}, u32[]{:S(2)}, u32[]{:S(2)}) %collective-permute-start.48) | collective-permute-done | bytes 360480 | tf_op jit(solution)/shard_map/ppermute | solution.py:50
  273.9 36.9 %attn_bwd.1.g_ref = bf16[2048,768]{1,0:T(8,128)(2,1)} custom-call(s32[1]{0:T(128)} %bitcast.me_ref, s32[1]{0:T(128)S(6)} %copy.57.count_ref, bf16[2048,768]{1,0:T(8,128)(2,1)} %get-tuple-element.83.qkv_ref, bf16[512,256]{1,0:T(8,128)(2,1)} %get-tuple-element.84.d0_ref, bf16[512,256]{1,0:T(8,128)(2,1)} %collective-permute-done.23.d1_ref, ...), custom_call_target="tpu_custom_call" | custom-call | flops 21474836480 | bytes 8388608 | tf_op jit(solution)/shard_map/attn_bwd/pallas_call | solution.py:250
  311.8 8.4 %wgrad_qkv.1 = bf16[8,128,1024]{2,1,0:T(8,128)(2,1)} custom-call(s32[1]{0:T(128)} %bitcast.me_ref, s32[1]{0:T(128)} %bitcast.8.dp_ref, bf16[2048,768]{1,0:T(8,128)(2,1)} %attn_bwd.1.g_ref, bf16[512,1024]{1,0:T(8,128)(2,1)} %fusion.2.a_ref.n0, bf16[512,1024]{1,0:T(8,128)(2,1)} %collective-permute-done.b_ref.n1, ...), custom_call_target="tpu_custom_call" | custom-call | flops 3221225472 | bytes 11010048 | tf_op jit(solution)/shard_map/wgrad_qkv/pallas_call | solution.py:553
  333.5 18.7 %collective-permute-done.50.p1 = bf16[1,704,128]{2,1,0:T(8,128)(2,1)S(1)} collective-permute-done((bf16[1,704,128]{2,1,0:T(8,128)(2,1)S(1)}, bf16[1,704,128]{2,1,0:T(8,128)(2,1)S(1)}, u32[]{:S(2)}, u32[]{:S(2)}) %collective-permute-start.50) | collective-permute-done | bytes 180256 | tf_op jit(solution)/shard_map/ppermute | solution.py:50
  366.8 7.6 %collective-permute-done.44.p1 = bf16[1,2,128,704]{3,2,1,0:T(8,128)(2,1)S(1)} collective-permute-done((bf16[1,2,128,704]{3,2,1,0:T(8,128)(2,1)S(1)}, bf16[1,2,128,704]{3,2,1,0:T(8,128)(2,1)S(1)}, u32[]{:S(2)}, u32[]{:S(2)}) %collective-permute-start.44) | collective-permute-done | bytes 360480 | tf_op jit(solution)/shard_map/ppermute | solution.py:50
  376.2 6.0 %collective-permute-done.36 = bf16[2,128,1024]{2,1,0:T(8,128)(2,1)} collective-permute-done((bf16[2,128,1024]{2,1,0:T(8,128)(2,1)}, bf16[2,128,1024]{2,1,0:T(8,128)(2,1)}, u32[]{:S(2)}, u32[]{:S(2)}) %collective-permute-start.36) | collective-permute-done | bytes 524320 | tf_op jit(solution)/shard_map/ppermute | solution.py:50
  389.1 13.2 %collective-permute-done.37 = bf16[1,128,1024]{2,1,0:T(8,128)(2,1)S(1)} collective-permute-done((bf16[1,128,1024]{2,1,0:T(8,128)(2,1)S(1)}, bf16[1,128,1024]{2,1,0:T(8,128)(2,1)S(1)}, u32[]{:S(2)}, u32[]{:S(2)}) %collective-permute-start.37) | collective-permute-done | bytes 262176 | tf_op jit(solution)/shard_map/ppermute | solution.py:50
  412.1 5.3 %grad_tokens.1 = (f32[512,1024]{1,0:T(8,128)}, f32[1,1024]{1,0:T(1,128)}) custom-call(f32[512,1024]{1,0:T(8,128)} %get-tuple-element.82.gm, bf16[512,1024]{1,0:T(8,128)(2,1)} %tok.1, bf16[512,1024]{1,0:T(8,128)(2,1)} %get-tuple-element.88.g0, bf16[512,1024]{1,0:T(8,128)(2,1)} %collective-permute-done.24.g1, bf16[512,1024]{1,0:T(8,128)(2,1)} %collective-permute-done.26.g2, ...), custom_call_target="tpu_custom_call" | custom-call | flops 10485760 | bytes 10485760 | tf_op jit(solution)/shard_map/grad_tokens/pallas_call | solution.py:411
  426.0 9.6 %collective-permute-done.28 = f32[2,1024]{1,0:T(2,128)S(1)} collective-permute-done((f32[2,1024]{1,0:T(2,128)S(1)}, f32[2,1024]{1,0:T(2,128)S(1)}, u32[]{:S(2)}, u32[]{:S(2)}) %collective-permute-start.28) | collective-permute-done | bytes 8224 | tf_op jit(solution)/shard_map/ppermute | solution.py:50
  438.8 22.1 %collective-permute-done.29 = f32[2,1024]{1,0:T(2,128)S(1)} collective-permute-done((f32[2,1024]{1,0:T(2,128)S(1)}, f32[2,1024]{1,0:T(2,128)S(1)}, u32[]{:S(2)}, u32[]{:S(2)}) %collective-permute-start.29) | collective-permute-done | bytes 8224 | tf_op jit(solution)/shard_map/ppermute | solution.py:50
  475.2 5.9 %finish_gate_up.1 = f32[1024,2,704]{2,1,0:T(2,128)} custom-call(s32[1]{0:T(128)} %bitcast.8.dp_ref, bf16[1,2,128,704]{3,2,1,0:T(8,128)(2,1)} %copy-done.1, bf16[1,2,128,704]{3,2,1,0:T(8,128)(2,1)} %copy-done.4, bf16[2,2,128,704]{3,2,1,0:T(8,128)(2,1)} %copy.47.p2, bf16[4,2,128,704]{3,2,1,0:T(8,128)(2,1)} %copy.48.p4), custom_call_target="tpu_custom_call" | custom-call | flops 1000000 | bytes 8650752 | tf_op jit(solution)/shard_map/finish_gate_up/pallas_call | solution.py:620
  481.1 10.1 %copy.50 = f32[1024,2,704]{0,2,1:T(8,128)} copy(f32[1024,2,704]{2,1,0:T(2,128)} %finish_gate_up.1) | data formatting | bytes 11534336
  (205 shorter events, 170.1 us)
Async XLA Ops:
  36.8 37.9 %collective-permute-start.6 = (bf16[256,1024]{1,0:T(8,128)(2,1)S(1)}, bf16[256,1024]{1,0:T(8,128)(2,1)S(1)}, u32[]{:S(2)}, u32[]{:S(2)}) collective-permute-start(bf16[256,1024]{1,0:T(8,128)(2,1)S(1)} %copy-done.11), channel_id=1, source_target_pairs={{0,1},{1,0},{2,3},{3,2},{4,5},{5,4},{6,7},{7,6},{8,9},{9,8},{10,11... | collective-permute-start | bytes 1572872 | tf_op jit(solution)/shard_map/ppermute | solution.py:50
  45.5 30.8 %collective-permute-start.8 = (bf16[256,1024]{1,0:T(8,128)(2,1)S(1)}, bf16[256,1024]{1,0:T(8,128)(2,1)S(1)}, u32[]{:S(2)}, u32[]{:S(2)}) collective-permute-start(bf16[256,1024]{1,0:T(8,128)(2,1)S(1)} %collective-permute-done.7.w2), channel_id=1, source_target_pairs={{0,1},{1,0},{2,3},{3,2},{4,5},{5,4},{6,7},{7,6},{8,9},{9,8},{10,11... | collective-permute-start | bytes 1572872 | tf_op jit(solution)/shard_map/ppermute | solution.py:50
  74.8 35.8 %collective-permute-start.14 = (bf16[512,1024]{1,0:T(8,128)(2,1)}, bf16[512,1024]{1,0:T(8,128)(2,1)}, u32[]{:S(2)}, u32[]{:S(2)}) collective-permute-start(bf16[512,1024]{1,0:T(8,128)(2,1)} %c0), channel_id=1, source_target_pairs={{0,2},{1,3},{2,0},{3,1},{4,6},{5,7},{6,4},{7,5},{8,10},{9,11},{10,... | collective-permute-start | bytes 3145736 | tf_op jit(solution)/shard_map/ppermute | solution.py:50
  93.6 38.7 %collective-permute-start.12 = (bf16[512,1024]{1,0:T(8,128)(2,1)}, bf16[512,1024]{1,0:T(8,128)(2,1)}, u32[]{:S(2)}, u32[]{:S(2)}) collective-permute-start(bf16[512,1024]{1,0:T(8,128)(2,1)} %get-tuple-element.66.na.n0), channel_id=1, source_target_pairs={{0,2},{1,3},{2,0},{3,1},{4,6},{5,7},{6,4},{7,5},{8,10},{9,11},{10,... | collective-permute-start | bytes 3145736 | tf_op jit(solution)/shard_map/ppermute | solution.py:50
  94.5 43.0 %collective-permute-start.10 = (bf16[512,1024]{1,0:T(8,128)(2,1)}, bf16[512,1024]{1,0:T(8,128)(2,1)}, u32[]{:S(2)}, u32[]{:S(2)}) collective-permute-start(bf16[512,1024]{1,0:T(8,128)(2,1)} %c0), channel_id=1, source_target_pairs={{0,1},{1,0},{2,3},{3,2},{4,5},{5,4},{6,7},{7,6},{8,9},{9,8},{10,11... | collective-permute-start | bytes 3145736 | tf_op jit(solution)/shard_map/ppermute | solution.py:50
  95.5 41.9 %collective-permute-start.9 = (bf16[512,1024]{1,0:T(8,128)(2,1)}, bf16[512,1024]{1,0:T(8,128)(2,1)}, u32[]{:S(2)}, u32[]{:S(2)}) collective-permute-start(bf16[512,1024]{1,0:T(8,128)(2,1)} %get-tuple-element.66.na.n0), channel_id=1, source_target_pairs={{0,1},{1,0},{2,3},{3,2},{4,5},{5,4},{6,7},{7,6},{8,9},{9,8},{10,11... | collective-permute-start | bytes 3145736 | tf_op jit(solution)/shard_map/ppermute | solution.py:50
  110.6 43.6 %collective-permute-start.15 = (bf16[512,1024]{1,0:T(8,128)(2,1)}, bf16[512,1024]{1,0:T(8,128)(2,1)}, u32[]{:S(2)}, u32[]{:S(2)}) collective-permute-start(bf16[512,1024]{1,0:T(8,128)(2,1)} %collective-permute-done.14.ca.c2), channel_id=1, source_target_pairs={{0,1},{1,0},{2,3},{3,2},{4,5},{5,4},{6,7},{7,6},{8,9},{9,8},{10,11... | collective-permute-start | bytes 3145736 | tf_op jit(solution)/shard_map/ppermute | solution.py:50
  186.0 34.4 %collective-permute-start.41 = (bf16[4,2,128,704]{2,3,1,0:T(8,128)(2,1)S(1)}, bf16[4,2,128,704]{2,3,1,0:T(8,128)(2,1)S(1)}, u32[]{:S(2)}, u32[]{:S(2)}) collective-permute-start(bf16[4,2,128,704]{2,3,1,0:T(8,128)(2,1)S(1)} %copy.38), channel_id=1, source_target_pairs={{0,4},{4,0},{8,12},{12,8},{16,20},{20,16},{24,28},{28,24},{1,5},{5... | collective-permute-start | bytes 4325384 | tf_op jit(solution)/shard_map/ppermute | solution.py:50
  188.0 51.0 %collective-permute-start.11 = (bf16[512,1024]{1,0:T(8,128)(2,1)}, bf16[512,1024]{1,0:T(8,128)(2,1)}, u32[]{:S(2)}, u32[]{:S(2)}) collective-permute-start(bf16[512,1024]{1,0:T(8,128)(2,1)} %get-tuple-element.70), channel_id=1, source_target_pairs={{0,1},{1,0},{2,3},{3,2},{4,5},{5,4},{6,7},{7,6},{8,9},{9,8},{10,11... | collective-permute-start | bytes 3145736 | tf_op jit(solution)/shard_map/ppermute | solution.py:50
  197.9 37.7 %collective-permute-start.47 = (bf16[4,704,128]{2,1,0:T(8,128)(2,1)}, bf16[4,704,128]{2,1,0:T(8,128)(2,1)}, u32[]{:S(2)}, u32[]{:S(2)}) collective-permute-start(bf16[4,704,128]{2,1,0:T(8,128)(2,1)} %slice.154), channel_id=1, source_target_pairs={{0,4},{4,0},{8,12},{12,8},{16,20},{20,16},{24,28},{28,24},{1,5},{5... | collective-permute-start | bytes 2162696 | tf_op jit(solution)/shard_map/ppermute | solution.py:50
  199.6 39.5 %collective-permute-start.17 = (bf16[512,1024]{1,0:T(8,128)(2,1)}, bf16[512,1024]{1,0:T(8,128)(2,1)}, u32[]{:S(2)}, u32[]{:S(2)}) collective-permute-start(bf16[512,1024]{1,0:T(8,128)(2,1)} %add_convert_fusion.2), channel_id=1, source_target_pairs={{0,2},{1,3},{2,0},{3,1},{4,6},{5,7},{6,4},{7,5},{8,10},{9,11},{10,... | collective-permute-start | bytes 3145736 | tf_op jit(solution)/shard_map/ppermute | solution.py:50
  230.8 30.4 %collective-permute-start.42 = (bf16[2,2,128,704]{2,3,1,0:T(8,128)(2,1)S(1)}, bf16[2,2,128,704]{2,3,1,0:T(8,128)(2,1)S(1)}, u32[]{:S(2)}, u32[]{:S(2)}) collective-permute-start(bf16[2,2,128,704]{2,3,1,0:T(8,128)(2,1)S(1)} %copy.41), channel_id=1, source_target_pairs={{0,8},{4,12},{8,0},{12,4},{16,24},{20,28},{24,16},{28,20},{1,9},{5... | collective-permute-start | bytes 2162696 | tf_op jit(solution)/shard_map/ppermute | solution.py:50
  256.9 72.9 %collective-permute-start.49 = (bf16[1,704,128]{2,1,0:T(8,128)(2,1)}, bf16[1,704,128]{2,1,0:T(8,128)(2,1)}, u32[]{:S(2)}, u32[]{:S(2)}) collective-permute-start(bf16[1,704,128]{2,1,0:T(8,128)(2,1)} %add_convert_fusion.17), channel_id=1, source_target_pairs={{0,16},{4,20},{8,24},{12,28},{16,0},{20,4},{24,8},{28,12},{1,17},{... | collective-permute-start | bytes 540680 | tf_op jit(solution)/shard_map/ppermute | solution.py:50
  262.1 48.7 %collective-permute-start.32 = (bf16[1024,256]{1,0:T(8,128)(2,1)}, bf16[1024,256]{1,0:T(8,128)(2,1)S(1)}, u32[]{:S(2)}, u32[]{:S(2)}) collective-permute-start(bf16[1024,256]{1,0:T(8,128)(2,1)} %get-tuple-element.97), channel_id=1, source_target_pairs={{0,1},{1,0},{2,3},{3,2},{4,5},{5,4},{6,7},{7,6},{8,9},{9,8},{10,11... | collective-permute-start | bytes 1572872 | tf_op jit(solution)/shard_map/ppermute | solution.py:50
  268.5 42.4 %collective-permute-start.34 = (bf16[1024,256]{1,0:T(8,128)(2,1)S(1)}, bf16[1024,256]{1,0:T(8,128)(2,1)S(1)}, u32[]{:S(2)}, u32[]{:S(2)}) collective-permute-start(bf16[1024,256]{1,0:T(8,128)(2,1)S(1)} %add_convert_fusion.7), channel_id=1, source_target_pairs={{0,2},{1,3},{2,0},{3,1},{4,6},{5,7},{6,4},{7,5},{8,10},{9,11},{10,... | collective-permute-start | bytes 1572872 | tf_op jit(solution)/shard_map/ppermute | solution.py:50
  322.6 32.6 %collective-permute-start.35 = (bf16[4,128,1024]{2,1,0:T(8,128)(2,1)}, bf16[4,128,1024]{2,1,0:T(8,128)(2,1)}, u32[]{:S(2)}, u32[]{:S(2)}) collective-permute-start(bf16[4,128,1024]{2,1,0:T(8,128)(2,1)} %slice.136), channel_id=1, source_target_pairs={{0,4},{4,0},{8,12},{12,8},{16,20},{20,16},{24,28},{28,24},{1,5},{5... | collective-permute-start | bytes 3145736 | tf_op jit(solution)/shard_map/ppermute | solution.py:50
  329.8 33.8 %collective-permute-start.25 = (bf16[512,1024]{1,0:T(8,128)(2,1)}, bf16[512,1024]{1,0:T(8,128)(2,1)}, u32[]{:S(2)}, u32[]{:S(2)}) collective-permute-start(bf16[512,1024]{1,0:T(8,128)(2,1)} %get-tuple-element.91), channel_id=1, source_target_pairs={{0,1},{1,0},{2,3},{3,2},{4,5},{5,4},{6,7},{7,6},{8,9},{9,8},{10,11... | collective-permute-start | bytes 3145736 | tf_op jit(solution)/shard_map/ppermute | solution.py:50
  352.9 69.0 %collective-permute-start.51 = (bf16[2,704,128]{2,1,0:T(8,128)(2,1)}, bf16[2,704,128]{2,1,0:T(8,128)(2,1)}, u32[]{:S(2)}, u32[]{:S(2)}) collective-permute-start(bf16[2,704,128]{2,1,0:T(8,128)(2,1)} %pad_maximum_fusion.5), channel_id=1, source_target_pairs={{0,8},{4,12},{8,0},{12,4},{16,24},{20,28},{24,16},{28,20},{1,9},{5... | collective-permute-start | bytes 1081352 | tf_op jit(solution)/shard_map/ppermute | solution.py:50
  353.1 30.4 %collective-permute-start.21 = (bf16[512,1024]{1,0:T(8,128)(2,1)}, bf16[512,1024]{1,0:T(8,128)(2,1)}, u32[]{:S(2)}, u32[]{:S(2)}) collective-permute-start(bf16[512,1024]{1,0:T(8,128)(2,1)} %get-tuple-element.81), channel_id=1, source_target_pairs={{0,1},{1,0},{2,3},{3,2},{4,5},{5,4},{6,7},{7,6},{8,9},{9,8},{10,11... | collective-permute-start | bytes 3145736 | tf_op jit(solution)/shard_map/ppermute | solution.py:50
  363.7 44.4 %collective-permute-start.24 = (bf16[512,1024]{1,0:T(8,128)(2,1)}, bf16[512,1024]{1,0:T(8,128)(2,1)}, u32[]{:S(2)}, u32[]{:S(2)}) collective-permute-start(bf16[512,1024]{1,0:T(8,128)(2,1)} %get-tuple-element.89), channel_id=1, source_target_pairs={{0,1},{1,0},{2,3},{3,2},{4,5},{5,4},{6,7},{7,6},{8,9},{9,8},{10,11... | collective-permute-start | bytes 3145736 | tf_op jit(solution)/shard_map/ppermute | solution.py:50
  374.4 37.2 %collective-permute-start.26 = (bf16[512,1024]{1,0:T(8,128)(2,1)}, bf16[512,1024]{1,0:T(8,128)(2,1)}, u32[]{:S(2)}, u32[]{:S(2)}) collective-permute-start(bf16[512,1024]{1,0:T(8,128)(2,1)} %add_convert_fusion), channel_id=1, source_target_pairs={{0,2},{1,3},{2,0},{3,1},{4,6},{5,7},{6,4},{7,5},{8,10},{9,11},{10,... | collective-permute-start | bytes 3145736 | tf_op jit(solution)/shard_map/ppermute | solution.py:50
  402.2 65.9 %collective-permute-start.20 = (bf16[512,1024]{1,0:T(8,128)(2,1)}, bf16[512,1024]{1,0:T(8,128)(2,1)}, u32[]{:S(2)}, u32[]{:S(2)}) collective-permute-start(bf16[512,1024]{1,0:T(8,128)(2,1)} %get-tuple-element.77), channel_id=1, source_target_pairs={{0,1},{1,0},{2,3},{3,2},{4,5},{5,4},{6,7},{7,6},{8,9},{9,8},{10,11... | collective-permute-start | bytes 3145736 | tf_op jit(solution)/shard_map/ppermute | solution.py:50
  408.1 60.1 %collective-permute-start.22 = (bf16[512,1024]{1,0:T(8,128)(2,1)}, bf16[512,1024]{1,0:T(8,128)(2,1)}, u32[]{:S(2)}, u32[]{:S(2)}) collective-permute-start(bf16[512,1024]{1,0:T(8,128)(2,1)} %add_convert_fusion.1), channel_id=1, source_target_pairs={{0,2},{1,3},{2,0},{3,1},{4,6},{5,7},{6,4},{7,5},{8,10},{9,11},{10,... | collective-permute-start | bytes 3145736 | tf_op jit(solution)/shard_map/ppermute | solution.py:50
  411.6 61.0 %collective-permute-start.46 = (bf16[4,2,128,704]{2,3,1,0:T(8,128)(2,1)}, bf16[4,2,128,704]{2,3,1,0:T(8,128)(2,1)}, u32[]{:S(2)}, u32[]{:S(2)}) collective-permute-start(bf16[4,2,128,704]{2,3,1,0:T(8,128)(2,1)} %pad_maximum_fusion), channel_id=1, source_target_pairs={{0,4},{4,0},{8,12},{12,8},{16,20},{20,16},{24,28},{28,24},{1,5},{5... | collective-permute-start | bytes 4325384 | tf_op jit(solution)/shard_map/ppermute | solution.py:50
  (56 other events, 918.0 us)
